TPU v7x, 128 devices: a whole 4x4x4 slice. The times are simulated.
128 devices in a mesh: tower: 2 (over core), dp: 64 (over z, x, y).
Axes of the slice: x: 4, y: 4, z: 4, core: 2. Of those that a mesh axis runs over, the one named last changes fastest.
Arguments:
- image_tokens: bfloat16 [1024, 50, 768], P(('tower', 'dp')), may hold values from -6 to 6
- image_first_gain: float32 [768], replicated, may hold values from 0.5 to 1.5
- image_first_shift: float32 [768], replicated, may hold values from -3 to 3
- image_joint_weight: bfloat16 [768, 2304], replicated, may hold values from -0.21875 to 0.21875
- image_output_weight: bfloat16 [768, 768], replicated, may hold values from -1.25 to 1.25
- image_second_gain: float32 [768], replicated, may hold values from 0.5 to 1.5
- image_second_shift: float32 [768], replicated, may hold values from -3 to 3
- image_widen_weight: bfloat16 [768, 3072], replicated, may hold values from -0.21875 to 0.21875
- image_narrow_weight: bfloat16 [3072, 768], replicated, may hold values from -0.109375 to 0.109375
- image_final_gain: float32 [768], replicated, may hold values from 0.5 to 1.5
- image_final_shift: float32 [768], replicated, may hold values from -3 to 3
- image_projection: bfloat16 [768, 512], replicated, may hold values from -0.21875 to 0.21875
- image_block_out_grad: bfloat16 [1024, 50, 768], P(('tower', 'dp')), may hold values from -0.00018310547 to 0.00018310547
- text_tokens: bfloat16 [1024, 77, 512], P(('tower', 'dp')), may hold values from -6 to 6
- caption_lengths: int32 [1024], P(('tower', 'dp')), may hold values from 5 to 77, as said below
- text_first_gain: float32 [512], replicated, may hold values from 0.5 to 1.5
- text_first_shift: float32 [512], replicated, may hold values from -3 to 3
- text_joint_weight: bfloat16 [512, 1536], replicated, may hold values from -0.25 to 0.25
- text_output_weight: bfloat16 [512, 512], replicated, may hold values from -1 to 1
- text_second_gain: float32 [512], replicated, may hold values from 0.5 to 1.5
- text_second_shift: float32 [512], replicated, may hold values from -3 to 3
- text_widen_weight: bfloat16 [512, 2048], replicated, may hold values from -0.25 to 0.25
- text_narrow_weight: bfloat16 [2048, 512], replicated, may hold values from -0.125 to 0.125
- text_final_gain: float32 [512], replicated, may hold values from 0.5 to 1.5
- text_final_shift: float32 [512], replicated, may hold values from -3 to 3
- text_projection: bfloat16 [512, 512], replicated, may hold values from -0.25 to 0.25
- text_block_out_grad: bfloat16 [1024, 77, 512], P(('tower', 'dp')), may hold values from -0.00024414062 to 0.00024414062
- log_scale: float32 [1], replicated, may hold values from 3.4 to 4.1
Outputs:
- loss: float32 [1], replicated
- image_embedding: bfloat16 [1024, 512], P(('tower', 'dp'))
- text_embedding: bfloat16 [1024, 512], P(('tower', 'dp'))
- image_tokens_grad: float32 [1024, 50, 768], P(('tower', 'dp'))
- image_first_gain_grad: float32 [768], P('dp')
- image_first_shift_grad: float32 [768], P('dp')
- image_joint_weight_grad: float32 [768, 2304], P('dp')
- image_output_weight_grad: float32 [768, 768], P('dp')
- image_second_gain_grad: float32 [768], P('dp')
- image_second_shift_grad: float32 [768], P('dp')
- image_widen_weight_grad: float32 [768, 3072], P('dp')
- image_narrow_weight_grad: float32 [3072, 768], P('dp')
- image_final_gain_grad: float32 [768], P('dp')
- image_final_shift_grad: float32 [768], P('dp')
- image_projection_grad: float32 [768, 512], P('dp')
- text_tokens_grad: float32 [1024, 77, 512], P(('tower', 'dp'))
- text_first_gain_grad: float32 [512], P('dp')
- text_first_shift_grad: float32 [512], P('dp')
- text_joint_weight_grad: float32 [512, 1536], P('dp')
- text_output_weight_grad: float32 [512, 512], P('dp')
- text_second_gain_grad: float32 [512], P('dp')
- text_second_shift_grad: float32 [512], P('dp')
- text_widen_weight_grad: float32 [512, 2048], P('dp')
- text_narrow_weight_grad: float32 [2048, 512], P('dp')
- text_final_gain_grad: float32 [512], P('dp')
- text_final_shift_grad: float32 [512], P('dp')
- text_projection_grad: float32 [512, 512], P('dp')
- log_scale_grad: float32 [1], replicated
Inputs may be any that keep to these rules, and one draw needn't show every extreme that they name: `caption_lengths`: each caption's end-of-text token stands at position length minus 1; some caption has 77 tokens and some has 5.
All inputs are finite; a program needn't handle non-finite values.
Results may differ from a plain program's by a relative error of at most 0.024.
Values may be sent and summed in bfloat16 or wider, within the bound.
No kernel may reach another device: no remote copies, remote signals or barrier semaphores. Data moves between devices by JAX's collectives and lax.ppermute only.
A program may use at most 256 MiB of HBM per device.

v0:
```python
import jax
import jax.numpy as jnp
from jax import lax
from jax.sharding import PartitionSpec as P

IMG_HEADS = 12
TXT_HEADS = 8


exact_precision = lax.Precision.HIGHEST


def contract_rows(left, right):
    return lax.dot_general(
        left, right, (((0,), (0,)), ((), ())), preferred_element_type=jnp.float32
    )


def contract_cols(left, right):
    return lax.dot_general(
        left, right, (((1,), (1,)), ((), ())), preferred_element_type=jnp.float32
    )


def layer_norm(values, gain, shift):
    centre = jnp.mean(values, axis=-1, keepdims=True)
    offset = values - centre
    inverse = lax.rsqrt(jnp.mean(offset * offset, axis=-1, keepdims=True) + 1e-05)
    normal = offset * inverse
    return (normal * gain + shift, normal, inverse)


def norm_back(upstream, gain, normal, inverse):
    scaled = upstream * gain
    inner = (
        scaled
        - jnp.mean(scaled, axis=-1, keepdims=True)
        - normal * jnp.mean(scaled * normal, axis=-1, keepdims=True)
    )
    width = upstream.shape[-1]
    flat_up = upstream.reshape(-1, width)
    return (
        inner * inverse,
        jnp.sum(flat_up * normal.reshape(-1, width), axis=0),
        jnp.sum(flat_up, axis=0),
    )


def block_forward(tokens, params, heads, causal):
    (
        first_gain,
        first_shift,
        joint_weight,
        output_weight,
        second_gain,
        second_shift,
        widen_weight,
        narrow_weight,
    ) = params
    batch, length, width = tokens.shape
    head_size = width // heads
    factor = head_size ** (-0.5)
    inputs = tokens.astype(jnp.float32)
    normed_one, normal_one, inverse_one = layer_norm(inputs, first_gain, first_shift)
    normed_one = normed_one.astype(jnp.bfloat16).reshape(batch * length, width)
    joint = jnp.dot(normed_one, joint_weight, preferred_element_type=jnp.float32).astype(
        jnp.bfloat16
    )
    joint = joint.reshape(batch, length, 3, heads, head_size)
    queries = joint[:, :, 0]
    keys_all = joint[:, :, 1]
    values_all = joint[:, :, 2]
    scores = (
        jnp.einsum("blhd,bmhd->bhlm", queries, keys_all, preferred_element_type=jnp.float32)
        * factor
    )
    if causal:
        place = jnp.arange(length)
        scores = jnp.where(place[None, :] <= place[:, None], scores, -1e30)
    peak = jnp.max(scores, axis=-1, keepdims=True)
    raised = jnp.exp(scores - peak)
    probs = raised / jnp.sum(raised, axis=-1, keepdims=True)
    probs_low = probs.astype(jnp.bfloat16)
    context = jnp.einsum(
        "bhlm,bmhd->blhd", probs_low, values_all, preferred_element_type=jnp.float32
    )
    context = context.astype(jnp.bfloat16).reshape(batch * length, width)
    mixed = inputs + jnp.dot(context, output_weight, preferred_element_type=jnp.float32).reshape(
        batch, length, width
    )
    normed_two, normal_two, inverse_two = layer_norm(mixed, second_gain, second_shift)
    normed_two = normed_two.astype(jnp.bfloat16).reshape(batch * length, width)
    widened = jnp.dot(normed_two, widen_weight, preferred_element_type=jnp.float32)
    active = (widened * jax.nn.sigmoid(1.702 * widened)).astype(jnp.bfloat16)
    output = mixed + jnp.dot(active, narrow_weight, preferred_element_type=jnp.float32).reshape(
        batch, length, width
    )
    kept = (
        normal_one,
        inverse_one,
        normed_one,
        queries,
        keys_all,
        values_all,
        probs,
        probs_low,
        context,
        normal_two,
        inverse_two,
        normed_two,
        widened,
        active,
    )
    return (output, kept)


def block_backward(upstream, kept, params, heads):
    (
        normal_one,
        inverse_one,
        normed_one,
        queries,
        keys_all,
        values_all,
        probs,
        probs_low,
        context,
        normal_two,
        inverse_two,
        normed_two,
        widened,
        active,
    ) = kept
    (
        first_gain,
        first_shift,
        joint_weight,
        output_weight,
        second_gain,
        second_shift,
        widen_weight,
        narrow_weight,
    ) = params
    batch, length, width = upstream.shape
    head_size = width // heads
    factor = head_size ** (-0.5)
    narrow_in = upstream.reshape(batch * length, width).astype(jnp.bfloat16)
    narrow_grad = contract_rows(active, narrow_in)
    active_grad = contract_cols(narrow_in, narrow_weight)
    sigma = jax.nn.sigmoid(1.702 * widened)
    widened_grad = (active_grad * (sigma + 1.702 * widened * sigma * (1.0 - sigma))).astype(
        jnp.bfloat16
    )
    widen_grad = contract_rows(normed_two, widened_grad)
    normed_two_grad = contract_cols(widened_grad, widen_weight).reshape(batch, length, width)
    mixed_part, second_gain_grad, second_shift_grad = norm_back(
        normed_two_grad, second_gain, normal_two, inverse_two
    )
    mixed_grad = upstream + mixed_part
    mixed_low = mixed_grad.reshape(batch * length, width).astype(jnp.bfloat16)
    output_grad = contract_rows(context, mixed_low)
    context_grad = (
        contract_cols(mixed_low, output_weight)
        .astype(jnp.bfloat16)
        .reshape(batch, length, heads, head_size)
    )
    probs_grad = jnp.einsum(
        "blhd,bmhd->bhlm", context_grad, values_all, preferred_element_type=jnp.float32
    )
    values_grad = jnp.einsum(
        "bhlm,blhd->bmhd", probs_low, context_grad, preferred_element_type=jnp.float32
    )
    scores_grad = probs * (probs_grad - jnp.sum(probs_grad * probs, axis=-1, keepdims=True))
    scores_grad = scores_grad.astype(jnp.bfloat16)
    queries_grad = (
        jnp.einsum("bhlm,bmhd->blhd", scores_grad, keys_all, preferred_element_type=jnp.float32)
        * factor
    )
    keys_grad = (
        jnp.einsum("bhlm,blhd->bmhd", scores_grad, queries, preferred_element_type=jnp.float32)
        * factor
    )
    joint_grad = (
        jnp.stack([queries_grad, keys_grad, values_grad], axis=2)
        .astype(jnp.bfloat16)
        .reshape(batch * length, 3 * width)
    )
    joint_weight_grad = contract_rows(normed_one, joint_grad)
    normed_one_grad = contract_cols(joint_grad, joint_weight).reshape(batch, length, width)
    input_part, first_gain_grad, first_shift_grad = norm_back(
        normed_one_grad, first_gain, normal_one, inverse_one
    )
    grads = (
        first_gain_grad,
        first_shift_grad,
        joint_weight_grad,
        output_grad,
        second_gain_grad,
        second_shift_grad,
        widen_grad,
        narrow_grad,
    )
    return (mixed_grad + input_part, grads)


def head_forward(pooled, gain, shift, projection):
    normed, normal, inverse = layer_norm(pooled, gain, shift)
    normed = normed.astype(jnp.bfloat16)
    raw = jnp.dot(normed, projection, preferred_element_type=jnp.float32)
    factor = lax.rsqrt(jnp.sum(raw * raw, axis=-1, keepdims=True) + 1e-06)
    return ((raw * factor).astype(jnp.bfloat16), (normal, inverse, normed, raw, factor))


def head_backward(unit_grad, kept, gain, projection):
    normal, inverse, normed, raw, factor = kept
    raw_grad = factor * unit_grad - raw * (factor * factor * factor) * jnp.sum(
        unit_grad * raw, axis=-1, keepdims=True
    )
    raw_grad = raw_grad.astype(jnp.bfloat16)
    projection_grad = contract_rows(normed, raw_grad)
    normed_grad = contract_cols(raw_grad, projection)
    pooled_grad, gain_grad, shift_grad = norm_back(normed_grad, gain, normal, inverse)
    return (pooled_grad, gain_grad, shift_grad, projection_grad)


def shards(
    image_tokens,
    image_first_gain,
    image_first_shift,
    image_joint_weight,
    image_output_weight,
    image_second_gain,
    image_second_shift,
    image_widen_weight,
    image_narrow_weight,
    image_final_gain,
    image_final_shift,
    image_projection,
    image_block_out_grad,
    text_tokens,
    caption_lengths,
    text_first_gain,
    text_first_shift,
    text_joint_weight,
    text_output_weight,
    text_second_gain,
    text_second_shift,
    text_widen_weight,
    text_narrow_weight,
    text_final_gain,
    text_final_shift,
    text_projection,
    text_block_out_grad,
    log_scale,
):
    image_params = (
        image_first_gain,
        image_first_shift,
        image_joint_weight,
        image_output_weight,
        image_second_gain,
        image_second_shift,
        image_widen_weight,
        image_narrow_weight,
    )
    text_params = (
        text_first_gain,
        text_first_shift,
        text_joint_weight,
        text_output_weight,
        text_second_gain,
        text_second_shift,
        text_widen_weight,
        text_narrow_weight,
    )
    pairs_dev, image_len, image_width = image_tokens.shape
    text_len = text_tokens.shape[1]
    image_out, image_kept = block_forward(image_tokens, image_params, IMG_HEADS, False)
    image_unit, image_head = head_forward(
        image_out[:, 0], image_final_gain, image_final_shift, image_projection
    )
    ends = caption_lengths - 1
    chooser = (jnp.arange(text_len)[None, :] == ends[:, None]).astype(jnp.float32)
    text_out, text_kept = block_forward(text_tokens, text_params, TXT_HEADS, True)
    text_pooled = jnp.sum(chooser[:, :, None] * text_out, axis=1)
    text_unit, text_head = head_forward(
        text_pooled, text_final_gain, text_final_shift, text_projection
    )
    all_images, all_texts = (
        lax.all_gather(image_unit, ("tower", "dp"), axis=0, tiled=True),
        lax.all_gather(text_unit, ("tower", "dp"), axis=0, tiled=True),
    )
    pairs = all_images.shape[0]
    scale = jnp.exp(log_scale[0])
    base = lax.axis_index(("tower", "dp")) * pairs_dev
    images_wide = all_images.astype(jnp.float32)
    texts_wide = all_texts.astype(jnp.float32)
    own = base + jnp.arange(pairs_dev)
    identity = (jnp.arange(pairs)[None, :] == own[:, None]).astype(jnp.float32)
    image_sims = scale * jnp.einsum(
        "ie,je->ij", image_unit, all_texts, preferred_element_type=jnp.float32
    )
    text_sims = scale * jnp.einsum(
        "je,ie->ji", text_unit, all_images, preferred_element_type=jnp.float32
    )
    row_local = jax.nn.logsumexp(image_sims, axis=1)
    column_local = jax.nn.logsumexp(text_sims, axis=1)
    diagonal = scale * jnp.sum(
        image_unit.astype(jnp.float32) * text_unit.astype(jnp.float32), axis=-1
    )
    row_totals, column_totals, diagonals = (
        lax.all_gather(row_local, ("tower", "dp"), axis=0, tiled=True),
        lax.all_gather(column_local, ("tower", "dp"), axis=0, tiled=True),
        lax.all_gather(diagonal, ("tower", "dp"), axis=0, tiled=True),
    )
    loss = (jnp.sum(row_totals) + jnp.sum(column_totals) - 2.0 * jnp.sum(diagonals)) / (2.0 * pairs)
    image_weight = (
        jnp.exp(image_sims - row_local[:, None])
        + jnp.exp(image_sims - column_totals[None, :])
        - 2.0 * identity
    ) / (2.0 * pairs)
    text_weight = (
        jnp.exp(text_sims - row_totals[None, :])
        + jnp.exp(text_sims - column_local[:, None])
        - 2.0 * identity
    ) / (2.0 * pairs)
    scale_grad = lax.psum(jnp.sum(image_weight * image_sims), ("tower", "dp"))
    text_unit_grad = scale * jnp.dot(text_weight, images_wide, precision=exact_precision)
    image_unit_grad = scale * jnp.dot(image_weight, texts_wide, precision=exact_precision)
    image_pooled_grad, image_final_gain_grad, image_final_shift_grad, image_projection_grad = (
        head_backward(image_unit_grad, image_head, image_final_gain, image_projection)
    )
    image_upstream = image_block_out_grad.astype(jnp.float32).at[:, 0].add(image_pooled_grad)
    image_input_grad, image_grads = block_backward(
        image_upstream, image_kept, image_params, IMG_HEADS
    )
    text_pooled_grad, text_final_gain_grad, text_final_shift_grad, text_projection_grad = (
        head_backward(text_unit_grad, text_head, text_final_gain, text_projection)
    )
    text_upstream = (
        text_block_out_grad.astype(jnp.float32) + chooser[:, :, None] * text_pooled_grad[:, None, :]
    )
    text_input_grad, text_grads = block_backward(text_upstream, text_kept, text_params, TXT_HEADS)
    local = (
        list(image_grads)
        + [image_final_gain_grad, image_final_shift_grad, image_projection_grad]
        + list(text_grads)
        + [text_final_gain_grad, text_final_shift_grad, text_projection_grad]
    )
    shared = (
        lax.psum_scatter(local[0], "dp", scatter_dimension=0, tiled=True),
        lax.psum_scatter(local[1], "dp", scatter_dimension=0, tiled=True),
        lax.psum_scatter(local[2], "dp", scatter_dimension=0, tiled=True),
        lax.psum_scatter(local[3], "dp", scatter_dimension=0, tiled=True),
        lax.psum_scatter(local[4], "dp", scatter_dimension=0, tiled=True),
        lax.psum_scatter(local[5], "dp", scatter_dimension=0, tiled=True),
        lax.psum_scatter(local[6], "dp", scatter_dimension=0, tiled=True),
        lax.psum_scatter(local[7], "dp", scatter_dimension=0, tiled=True),
        lax.psum_scatter(local[8], "dp", scatter_dimension=0, tiled=True),
        lax.psum_scatter(local[9], "dp", scatter_dimension=0, tiled=True),
        lax.psum_scatter(local[10], "dp", scatter_dimension=0, tiled=True),
        lax.psum_scatter(local[11], "dp", scatter_dimension=0, tiled=True),
        lax.psum_scatter(local[12], "dp", scatter_dimension=0, tiled=True),
        lax.psum_scatter(local[13], "dp", scatter_dimension=0, tiled=True),
        lax.psum_scatter(local[14], "dp", scatter_dimension=0, tiled=True),
        lax.psum_scatter(local[15], "dp", scatter_dimension=0, tiled=True),
        lax.psum_scatter(local[16], "dp", scatter_dimension=0, tiled=True),
        lax.psum_scatter(local[17], "dp", scatter_dimension=0, tiled=True),
        lax.psum_scatter(local[18], "dp", scatter_dimension=0, tiled=True),
        lax.psum_scatter(local[19], "dp", scatter_dimension=0, tiled=True),
        lax.psum_scatter(local[20], "dp", scatter_dimension=0, tiled=True),
        lax.psum_scatter(local[21], "dp", scatter_dimension=0, tiled=True),
    )
    summed = (
        lax.psum(shared[0].astype(jnp.bfloat16), "tower").astype(jnp.float32),
        lax.psum(shared[1].astype(jnp.bfloat16), "tower").astype(jnp.float32),
        lax.psum(shared[2].astype(jnp.bfloat16), "tower").astype(jnp.float32),
        lax.psum(shared[3].astype(jnp.bfloat16), "tower").astype(jnp.float32),
        lax.psum(shared[4].astype(jnp.bfloat16), "tower").astype(jnp.float32),
        lax.psum(shared[5].astype(jnp.bfloat16), "tower").astype(jnp.float32),
        lax.psum(shared[6].astype(jnp.bfloat16), "tower").astype(jnp.float32),
        lax.psum(shared[7].astype(jnp.bfloat16), "tower").astype(jnp.float32),
        lax.psum(shared[8].astype(jnp.bfloat16), "tower").astype(jnp.float32),
        lax.psum(shared[9].astype(jnp.bfloat16), "tower").astype(jnp.float32),
        lax.psum(shared[10].astype(jnp.bfloat16), "tower").astype(jnp.float32),
        lax.psum(shared[11].astype(jnp.bfloat16), "tower").astype(jnp.float32),
        lax.psum(shared[12].astype(jnp.bfloat16), "tower").astype(jnp.float32),
        lax.psum(shared[13].astype(jnp.bfloat16), "tower").astype(jnp.float32),
        lax.psum(shared[14].astype(jnp.bfloat16), "tower").astype(jnp.float32),
        lax.psum(shared[15].astype(jnp.bfloat16), "tower").astype(jnp.float32),
        lax.psum(shared[16].astype(jnp.bfloat16), "tower").astype(jnp.float32),
        lax.psum(shared[17].astype(jnp.bfloat16), "tower").astype(jnp.float32),
        lax.psum(shared[18].astype(jnp.bfloat16), "tower").astype(jnp.float32),
        lax.psum(shared[19].astype(jnp.bfloat16), "tower").astype(jnp.float32),
        lax.psum(shared[20].astype(jnp.bfloat16), "tower").astype(jnp.float32),
        lax.psum(shared[21].astype(jnp.bfloat16), "tower").astype(jnp.float32),
    )
    return (
        loss.reshape(1),
        image_unit,
        text_unit,
        image_input_grad,
        summed[0],
        summed[1],
        summed[2],
        summed[3],
        summed[4],
        summed[5],
        summed[6],
        summed[7],
        summed[8],
        summed[9],
        summed[10],
        text_input_grad,
        summed[11],
        summed[12],
        summed[13],
        summed[14],
        summed[15],
        summed[16],
        summed[17],
        summed[18],
        summed[19],
        summed[20],
        summed[21],
        jnp.reshape(scale_grad, (1,)),
    )


def solution(mesh):
    placed = (
        P(("tower", "dp"), None, None),
        P(),
        P(),
        P(),
        P(),
        P(),
        P(),
        P(),
        P(),
        P(),
        P(),
        P(),
        P(("tower", "dp"), None, None),
        P(("tower", "dp"), None, None),
        P(("tower", "dp")),
        P(),
        P(),
        P(),
        P(),
        P(),
        P(),
        P(),
        P(),
        P(),
        P(),
        P(),
        P(("tower", "dp"), None, None),
        P(),
    )
    return jax.shard_map(
        shards,
        mesh=mesh,
        in_specs=placed,
        out_specs=(
            P(),
            P(("tower", "dp"), None),
            P(("tower", "dp"), None),
            P(("tower", "dp"), None, None),
            P("dp"),
            P("dp"),
            P("dp", None),
            P("dp", None),
            P("dp"),
            P("dp"),
            P("dp", None),
            P("dp", None),
            P("dp"),
            P("dp"),
            P("dp", None),
            P(("tower", "dp"), None, None),
            P("dp"),
            P("dp"),
            P("dp", None),
            P("dp", None),
            P("dp"),
            P("dp"),
            P("dp", None),
            P("dp", None),
            P("dp"),
            P("dp"),
            P("dp", None),
            P(),
        ),
        check_vma=False,
    )
```

profile of v0, /device:TPU:1, one launch (start us, length us, event | category | flops | bytes accessed | tf_op | source)
XLA Modules:
  0.0 2284.0 jit_solution(4119710836000555412)
XLA Ops:
  22.5 4.0 convolution_convert_fusion.1
  26.6 6.0 reshape.479
  32.5 4.1 fusion.108
  44.5 4.8 fusion.114
  57.0 4.0 convolution_convert_fusion
  61.0 6.7 reshape.432
  67.6 3.4 fusion.107
  72.8 4.5 fusion.120
  83.5 3.8 fusion.121
  94.5 7.3 multiply_convert_fusion.3
  103.3 5.4 fusion.124
  113.8 6.1 multiply_convert_fusion.1
  144.0 54.9 %all-gather.5.cloned.1.call-done = bf16[1024,512]{1,0:T(8,128)(2,1)} async-done(((bf16[8,512]{1,0:T(8,128)(2,1)}), bf16[1024,512]{1,0:T(8,128)(2,1)}) %all-gather.5.cloned.1.call-update) | async-done | bytes 1048592 | tf_op jit(solution)/shard_map/all_gather | solution.py:290
  203.3 62.7 %all-reduce.1 = f32[1024]{0:T(1024)} all-reduce(f32[1024]{0:T(1024)} %get-tuple-element.249), channel_id=1, replica_groups=mesh['tower'=2,'dp'=64] {'tower','dp'}, use_global_device_ids=true, to_apply=%add.1 | all-reduce | flops 1024 | bytes 8192
  269.8 64.5 %all-reduce.23 = (f32[1024]{0:T(1024)}, f32[1024]{0:T(1024)}, f32[1]{0:T(128)}) all-reduce(f32[1024]{0:T(1024)} %copy-done.96, f32[1024]{0:T(1024)} %multiply_dynamic-update-slice_fusion, f32[1]{0:T(128)} %bitcast.27), channel_id=1, replica_groups=mesh['tower'=2,'dp'=64] {'tower','dp'}, use_global_device_ids=true, to_apply=%add | all-reduce | flops 2049 | bytes 16392
  347.8 5.8 multiply_convert_fusion
  388.1 4.5 copy.249
  392.6 5.8 convert_element_type.358
  398.4 4.9 fusion.131
  403.4 5.8 fusion.133
  409.3 5.7 fusion.134
  443.0 8.1 fusion.129
  451.1 6.9 multiply_convert_fusion.2
  459.4 6.2 fusion.99
  503.1 7.3 convert_element_type.325
  515.2 5.0 fusion.126
  520.2 5.1 fusion.128
  525.3 311.1 %fusion.101 = (f32[16,2304]{1,0:T(8,128)}, f32[16,768]{1,0:T(8,128)}, f32[16,512]{1,0:T(8,128)}, f32[16,3072]{1,0:T(8,128)}) fusion(f32[768,2304]{1,0:T(8,128)} %fusion.126, f32[768,768]{1,0:T(8,128)} %fusion.127, f32[768,512]{1,0:T(8,128)} %fusion.90, f32[768,3072]{1,0:T(8,128)} %fusion.128), kind=kCustom, calls=%all-reduce-scatter.4 | all-reduce-scatter fusion | flops 6815745 | bytes 20873728
  848.3 5.2 fusion.100
  853.5 8.9 collective-permute-start.53
  864.3 6.5 collective-permute-start.55
  915.3 4.0 collective-permute-start.21
  919.4 4.0 collective-permute-start.22
  949.6 3.9 collective-permute-start.1
  953.5 4.0 multiply_add_fusion
  965.6 3.4 collective-permute-start.5
  995.0 288.0 %all-reduce.24 = (bf16[768]{0:T(1024)(128)(2,1)}, bf16[768]{0:T(1024)(128)(2,1)}, bf16[768]{0:T(1024)(128)(2,1)}, bf16[768]{0:T(1024)(128)(2,1)}, bf16[768]{0:T(...) all-reduce(f32[768]{0:T(1024)} %get-tuple-element.192, ...), channel_id=2, replica_groups=mesh['tower'=2,'dp'=64] {'dp'}, use_global_device_ids=true, to_apply=%region_36.37.clone | all-reduce | flops 7680 | bytes 46080
  1298.7 23.8 %concatenate.5 = bf16[268,512]{1,0:T(8,128)(2,1)} concatenate(bf16[12,512]{1,0:T(8,128)(2,1)} %collective-permute-done.63, bf16[16,512]{1,0:T(8,128)(2,1)} %collective-permute-done.62, bf16[16,512]{1,0:T(8,128)(2,1)} %copy-done.95, bf16[16,512]{1,0:T(8,128)(2,1)} %copy-done.94, bf16[16,512]{1,0:T(8,128)(2,1)} %copy-done.93, bf16[16,512]{1,0:T(8,128)(2,1)} %copy-done.92, ...), dimensions={0} | concatenate | bytes 565248
  1333.6 24.2 %concatenate.3 = bf16[268,768]{1,0:T(8,128)(2,1)} concatenate(bf16[12,768]{1,0:T(8,128)(2,1)} %collective-permute-done.31, bf16[16,768]{1,0:T(8,128)(2,1)} %collective-permute-done.30, bf16[16,768]{1,0:T(8,128)(2,1)} %collective-permute-done.29, bf16[16,768]{1,0:T(8,128)(2,1)} %collective-permute-done.28, bf16[16,768]{1,0:T(8,128)(2,1)} %collective-permute-done.27, ...), dimensions={0} | concatenate | bytes 847872
  1365.5 16.9 collective-permute-start.42
  1383.7 28.0 %concatenate.2 = bf16[268,2304]{1,0:T(8,128)(2,1)} concatenate(bf16[12,2304]{1,0:T(8,128)(2,1)} %collective-permute-done.15, bf16[16,2304]{1,0:T(8,128)(2,1)} %collective-permute-done.14, bf16[16,2304]{1,0:T(8,128)(2,1)} %collective-permute-done.13, bf16[16,2304]{1,0:T(8,128)(2,1)} %collective-permute-done.12, bf16[16,2304]{1,0:T(8,128)(2,1)} %copy-done.67, ...), dimensions={0} | concatenate | bytes 2543616
  1424.1 40.1 %concatenate.4 = bf16[268,3072]{1,0:T(8,128)(2,1)} concatenate(bf16[12,3072]{1,0:T(8,128)(2,1)} %collective-permute-done.47, bf16[16,3072]{1,0:T(8,128)(2,1)} %collective-permute-done.46, bf16[16,3072]{1,0:T(8,128)(2,1)} %collective-permute-done.45, bf16[16,3072]{1,0:T(8,128)(2,1)} %collective-permute-done.44, bf16[16,3072]{1,0:T(8,128)(2,1)} %collective-permute-done.43, ...), dimensions={0} | concatenate | bytes 3391488
  1468.2 112.3 %reduce-scatter.21.cloned.1.call-done = f32[8,2048]{1,0:T(8,128)} async-done(((f32[512,2048]{1,0:T(8,128)}), f32[8,2048]{1,0:T(8,128)}) %reduce-scatter.21.cloned.1.call-update) | async-done | bytes 65552 | tf_op jit(solution)/shard_map/reduce_scatter | solution.py:368
  1582.0 354.3 %reduce-scatter.23.cloned.1.call-done = f32[32,512]{1,0:T(8,128)} async-done(((f32[2048,512]{1,0:T(8,128)}), f32[32,512]{1,0:T(8,128)}) %reduce-scatter.23.cloned.1.call-update) | async-done | bytes 65552 | tf_op jit(solution)/shard_map/reduce_scatter | solution.py:369
  1939.4 271.4 %reduce-scatter.15.cloned.1.call-done = f32[48,768]{1,0:T(8,128)} async-done(((f32[3072,768]{1,0:T(8,128)}), f32[48,768]{1,0:T(8,128)}) %reduce-scatter.15.cloned.1.call-update) | async-done | bytes 147472 | tf_op jit(solution)/shard_map/reduce_scatter | solution.py:358
  2212.4 3.5 multiply_add_fusion.3
  2222.8 21.3 all-reduce.31.cloned.1.call-done
  2268.9 3.6 all-reduce.33.cloned.1.call-done
  (605 shorter events, 410.3 us)
Async XLA Ops:
  7.2 191.6 %all-gather.5.cloned.1.call-start = ((), (), s32[]{:S(2)}) async-start(), calls=%async_computation.7 | async-start | bytes 1056768 | tf_op jit(solution)/shard_map/all_gather | solution.py:290
  131.5 134.5 %all-gather.3.cloned.1.call-start = ((), (), s32[]{:S(2)}) async-start(), calls=%async_computation.6 | async-start | bytes 1056768 | tf_op jit(solution)/shard_map/all_gather | solution.py:291
  132.2 1331.9 %reduce-scatter.25.cloned.1.call-start = ((), (), s32[]{:S(2)}) async-start(), calls=%async_computation.13 | async-start | bytes 1064960 | tf_op jit(solution)/shard_map/reduce_scatter | solution.py:372
  347.7 1117.8 %reduce-scatter.19.cloned.1.call-start = ((), (), s32[]{:S(2)}) async-start(), calls=%async_computation.10 | async-start | bytes 1064960 | tf_op jit(solution)/shard_map/reduce_scatter | solution.py:365
  379.5 1087.3 %reduce-scatter.17.cloned.1.call-start = ((), (), s32[]{:S(2)}) async-start(), calls=%async_computation.9 | async-start | bytes 3194880 | tf_op jit(solution)/shard_map/reduce_scatter | solution.py:364
  403.3 1177.2 %reduce-scatter.21.cloned.1.call-start = ((), (), s32[]{:S(2)}) async-start(), calls=%async_computation.11 | async-start | bytes 4259840 | tf_op jit(solution)/shard_map/reduce_scatter | solution.py:368
  409.2 1527.1 %reduce-scatter.23.cloned.1.call-start = ((), (), s32[]{:S(2)}) async-start(), calls=%async_computation.12 | async-start | bytes 4259840 | tf_op jit(solution)/shard_map/reduce_scatter | solution.py:369
  415.0 1795.9 %reduce-scatter.15.cloned.1.call-start = ((), (), s32[]{:S(2)}) async-start(), calls=%async_computation.8 | async-start | bytes 9584640 | tf_op jit(solution)/shard_map/reduce_scatter | solution.py:358
  465.7 1778.5 %all-reduce.31.cloned.1.call-start = ((), (), s32[]{:S(2)}) async-start(), calls=%async_computation.14 | async-start | bytes 454656 | tf_op jit(solution)/shard_map/psum | solution.py:375
  838.5 23.9 %collective-permute-start.49 = (bf16[16,512]{1,0:T(8,128)(2,1)}, bf16[16,512]{1,0:T(8,128)(2,1)}, u32[]{:S(2)}, u32[]{:S(2)}) collective-permute-start(bf16[16,512]{1,0:T(8,128)(2,1)} %convert.123), channel_id=1, source_target_pairs={{0,2},{1,3},{2,4},{3,5},{4,6},{5,7},{6,8},{7,9},{8,10},{9,11},{10,... | collective-permute-start | bytes 49160
  840.6 23.6 %collective-permute-start.50 = (bf16[16,512]{1,0:T(8,128)(2,1)}, bf16[16,512]{1,0:T(8,128)(2,1)}, u32[]{:S(2)}, u32[]{:S(2)}) collective-permute-start(bf16[16,512]{1,0:T(8,128)(2,1)} %convert.123), channel_id=1, source_target_pairs={{0,3},{1,4},{2,5},{3,6},{4,7},{5,8},{6,9},{7,10},{8,11},{9,12},{10... | collective-permute-start | bytes 49160
  842.5 28.2 %collective-permute-start.51 = (bf16[16,512]{1,0:T(8,128)(2,1)}, bf16[16,512]{1,0:T(8,128)(2,1)}, u32[]{:S(2)}, u32[]{:S(2)}) collective-permute-start(bf16[16,512]{1,0:T(8,128)(2,1)} %convert.123), channel_id=1, source_target_pairs={{0,4},{1,5},{2,6},{3,7},{4,8},{5,9},{6,10},{7,11},{8,12},{9,13},{1... | collective-permute-start | bytes 49160
  844.4 34.3 %collective-permute-start.52 = (bf16[16,512]{1,0:T(8,128)(2,1)}, bf16[16,512]{1,0:T(8,128)(2,1)}, u32[]{:S(2)}, u32[]{:S(2)}) collective-permute-start(bf16[16,512]{1,0:T(8,128)(2,1)} %convert.123), channel_id=1, source_target_pairs={{0,5},{1,6},{2,7},{3,8},{4,9},{5,10},{6,11},{7,12},{8,13},{9,14},{... | collective-permute-start | bytes 49160
  853.5 28.2 %collective-permute-start.53 = (bf16[16,512]{1,0:T(8,128)(2,1)}, bf16[16,512]{1,0:T(8,128)(2,1)}, u32[]{:S(2)}, u32[]{:S(2)}) collective-permute-start(bf16[16,512]{1,0:T(8,128)(2,1)} %convert.123), channel_id=1, source_target_pairs={{0,6},{1,7},{2,8},{3,9},{4,10},{5,11},{6,12},{7,13},{8,14},{9,15},... | collective-permute-start | bytes 49160
  862.4 22.1 collective-permute-start.54
  864.3 22.5 collective-permute-start.55
  870.7 17.4 collective-permute-start.56
  878.7 15.8 collective-permute-start.57
  881.7 15.5 collective-permute-start.58
  886.8 15.3 collective-permute-start.60
  888.1 17.2 collective-permute-start.61
  894.5 15.9 collective-permute-start.62
  899.6 19.8 collective-permute-start.17
  902.1 21.3 collective-permute-start.18
  910.4 17.6 collective-permute-start.19
  912.5 17.4 collective-permute-start.20
  915.3 16.8 collective-permute-start.21
  941.0 19.1 collective-permute-start.29
  942.9 18.9 collective-permute-start.30
  944.8 18.6 collective-permute-start.16
  947.6 17.9 collective-permute-start.15
  949.6 19.4 collective-permute-start.1
  983.3 339.2 %collective-permute-start.12 = (bf16[16,2304]{1,0:T(8,128)(2,1)}, bf16[16,2304]{1,0:T(8,128)(2,1)}, u32[]{:S(2)}, u32[]{:S(2)}) collective-permute-start(bf16[16,2304]{1,0:T(8,128)(2,1)} %convert.121), channel_id=1, source_target_pairs={{0,13},{1,14},{2,15},{3,16},{4,17},{5,18},{6,19},{7,20},{8,21},{9,... | collective-permute-start | bytes 221192
  985.9 338.6 %collective-permute-start.13 = (bf16[16,2304]{1,0:T(8,128)(2,1)}, bf16[16,2304]{1,0:T(8,128)(2,1)}, u32[]{:S(2)}, u32[]{:S(2)}) collective-permute-start(bf16[16,2304]{1,0:T(8,128)(2,1)} %convert.121), channel_id=1, source_target_pairs={{0,14},{1,15},{2,16},{3,17},{4,18},{5,19},{6,20},{7,21},{8,22},{9,... | collective-permute-start | bytes 221192
  987.8 338.6 %collective-permute-start.14 = (bf16[16,2304]{1,0:T(8,128)(2,1)}, bf16[16,2304]{1,0:T(8,128)(2,1)}, u32[]{:S(2)}, u32[]{:S(2)}) collective-permute-start(bf16[16,2304]{1,0:T(8,128)(2,1)} %convert.121), channel_id=1, source_target_pairs={{0,15},{1,16},{2,17},{3,18},{4,19},{5,20},{6,21},{7,22},{8,23},{9,... | collective-permute-start | bytes 221192
  989.7 338.6 %collective-permute-start = (bf16[16,2304]{1,0:T(8,128)(2,1)}, bf16[16,2304]{1,0:T(8,128)(2,1)}, u32[]{:S(2)}, u32[]{:S(2)}) collective-permute-start(bf16[16,2304]{1,0:T(8,128)(2,1)} %convert.121), channel_id=1, source_target_pairs={{0,1},{1,2},{2,3},{3,4},{4,5},{5,6},{6,7},{7,8},{8,9},{9,10},{10,1... | collective-permute-start | bytes 221192
  992.3 338.0 %collective-permute-start.47 = (bf16[12,3072]{1,0:T(8,128)(2,1)}, bf16[12,3072]{1,0:T(8,128)(2,1)}, u32[]{:S(2)}, u32[]{:S(2)}) collective-permute-start(bf16[12,3072]{1,0:T(8,128)(2,1)} %slice.62), channel_id=1, source_target_pairs={{0,16},{1,17},{2,18},{3,19},{4,20},{5,21},{6,22},{7,23},{8,24},{9,... | collective-permute-start | bytes 221192
  1322.6 35.2 %collective-permute-start.33 = (bf16[16,3072]{1,0:T(8,128)(2,1)}, bf16[16,3072]{1,0:T(8,128)(2,1)}, u32[]{:S(2)}, u32[]{:S(2)}) collective-permute-start(bf16[16,3072]{1,0:T(8,128)(2,1)} %convert.120), channel_id=1, source_target_pairs={{0,2},{1,3},{2,4},{3,5},{4,6},{5,7},{6,8},{7,9},{8,10},{9,11},{10,... | collective-permute-start | bytes 294920
  1324.5 35.2 %collective-permute-start.34 = (bf16[16,3072]{1,0:T(8,128)(2,1)}, bf16[16,3072]{1,0:T(8,128)(2,1)}, u32[]{:S(2)}, u32[]{:S(2)}) collective-permute-start(bf16[16,3072]{1,0:T(8,128)(2,1)} %convert.120), channel_id=1, source_target_pairs={{0,3},{1,4},{2,5},{3,6},{4,7},{5,8},{6,9},{7,10},{8,11},{9,12},{10... | collective-permute-start | bytes 294920
  1326.4 35.2 %collective-permute-start.35 = (bf16[16,3072]{1,0:T(8,128)(2,1)}, bf16[16,3072]{1,0:T(8,128)(2,1)}, u32[]{:S(2)}, u32[]{:S(2)}) collective-permute-start(bf16[16,3072]{1,0:T(8,128)(2,1)} %convert.120), channel_id=1, source_target_pairs={{0,4},{1,5},{2,6},{3,7},{4,8},{5,9},{6,10},{7,11},{8,12},{9,13},{1... | collective-permute-start | bytes 294920
  1328.4 35.2 %collective-permute-start.36 = (bf16[16,3072]{1,0:T(8,128)(2,1)}, bf16[16,3072]{1,0:T(8,128)(2,1)}, u32[]{:S(2)}, u32[]{:S(2)}) collective-permute-start(bf16[16,3072]{1,0:T(8,128)(2,1)} %convert.120), channel_id=1, source_target_pairs={{0,5},{1,6},{2,7},{3,8},{4,9},{5,10},{6,11},{7,12},{8,13},{9,14},{... | collective-permute-start | bytes 294920
  1330.3 35.2 %collective-permute-start.37 = (bf16[16,3072]{1,0:T(8,128)(2,1)}, bf16[16,3072]{1,0:T(8,128)(2,1)}, u32[]{:S(2)}, u32[]{:S(2)}) collective-permute-start(bf16[16,3072]{1,0:T(8,128)(2,1)} %convert.120), channel_id=1, source_target_pairs={{0,6},{1,7},{2,8},{3,9},{4,10},{5,11},{6,12},{7,13},{8,14},{9,15},... | collective-permute-start | bytes 294920
  1357.8 54.0 %collective-permute-start.38 = (bf16[16,3072]{1,0:T(8,128)(2,1)}, bf16[16,3072]{1,0:T(8,128)(2,1)}, u32[]{:S(2)}, u32[]{:S(2)}) collective-permute-start(bf16[16,3072]{1,0:T(8,128)(2,1)} %convert.120), channel_id=1, source_target_pairs={{0,7},{1,8},{2,9},{3,10},{4,11},{5,12},{6,13},{7,14},{8,15},{9,16}... | collective-permute-start | bytes 294920
  1359.7 54.0 %collective-permute-start.39 = (bf16[16,3072]{1,0:T(8,128)(2,1)}, bf16[16,3072]{1,0:T(8,128)(2,1)}, u32[]{:S(2)}, u32[]{:S(2)}) collective-permute-start(bf16[16,3072]{1,0:T(8,128)(2,1)} %convert.120), channel_id=1, source_target_pairs={{0,8},{1,9},{2,10},{3,11},{4,12},{5,13},{6,14},{7,15},{8,16},{9,17... | collective-permute-start | bytes 294920
  1361.7 54.0 %collective-permute-start.40 = (bf16[16,3072]{1,0:T(8,128)(2,1)}, bf16[16,3072]{1,0:T(8,128)(2,1)}, u32[]{:S(2)}, u32[]{:S(2)}) collective-permute-start(bf16[16,3072]{1,0:T(8,128)(2,1)} %convert.120), channel_id=1, source_target_pairs={{0,9},{1,10},{2,11},{3,12},{4,13},{5,14},{6,15},{7,16},{8,17},{9,1... | collective-permute-start | bytes 294920
  1363.6 54.0 %collective-permute-start.41 = (bf16[16,3072]{1,0:T(8,128)(2,1)}, bf16[16,3072]{1,0:T(8,128)(2,1)}, u32[]{:S(2)}, u32[]{:S(2)}) collective-permute-start(bf16[16,3072]{1,0:T(8,128)(2,1)} %convert.120), channel_id=1, source_target_pairs={{0,10},{1,11},{2,12},{3,13},{4,14},{5,15},{6,16},{7,17},{8,18},{9,... | collective-permute-start | bytes 294920
  1365.5 54.0 %collective-permute-start.42 = (bf16[16,3072]{1,0:T(8,128)(2,1)}, bf16[16,3072]{1,0:T(8,128)(2,1)}, u32[]{:S(2)}, u32[]{:S(2)}) collective-permute-start(bf16[16,3072]{1,0:T(8,128)(2,1)} %convert.120), channel_id=1, source_target_pairs={{0,11},{1,12},{2,13},{3,14},{4,15},{5,16},{6,17},{7,18},{8,19},{9,... | collective-permute-start | bytes 294920
  1937.8 334.7 %all-reduce.33.cloned.1.call-start = ((), (), s32[]{:S(2)}) async-start(), calls=%async_computation.15 | async-start | bytes 344064 | tf_op jit(solution)/shard_map/psum | solution.py:381
  (153 other events, 1269.4 us)
Sparse Core Ops, SparseCore 0:
  131.6 67.1 all-gather.4
  202.2 61.0 all-gather.2
  347.8 304.7 reduce-scatter.24
  654.9 352.4 reduce-scatter.18
  1011.6 259.4 reduce-scatter.16
  1273.4 307.1 reduce-scatter.20
  1583.0 353.2 reduce-scatter.22
  1940.9 269.9 reduce-scatter.14
  2217.6 26.4 all-reduce.30
  2247.2 25.2 all-reduce.32
where the time goes:
time: 2300 us; the launch traced here: 2280 us
  waiting for transfers between devices  819 us (36%)
  blocking collectives  726 us (32%)
  local copies, waits for them, and re-layouts  288 us (13%)
  starting transfers between devices  168 us (7%)
  matrix products  146 us (6%)
  other arithmetic  115 us (5%)
    unnamed x4, blocking collectives  726 us
    reduce_scatter x1, waiting for transfers between devices, shards(): lax.psum_scatter(local[18], 'dp', scatter_dimension=0, tiled=True)  354 us
    reduce_scatter x1, waiting for transfers between devices, shards(): lax.psum_scatter(local[7], 'dp', scatter_dimension=0, tiled=True)  271 us
    unnamed x64, starting transfers between devices  167 us
    unnamed x282, local copies, waits for them, and re-layouts  161 us
    reduce_scatter x1, waiting for transfers between devices, shards(): lax.psum_scatter(local[17], 'dp', scatter_dimension=0, tiled=True)  112 us
    all_gather x1, waiting for transfers between devices, shards(): lax.all_gather(image_unit, ('tower', 'dp'), axis=0, tiled=True)  54.9 us
  transfers between devices with their start and end apart: 74, of which 7 were waited for; matrix products, arithmetic and copies ran while one was open for 31% of the time, Pallas kernels for 0%

commit v1 on v0

v1 whole, which is shorter than its diff:
```python
import functools

import jax
import jax.numpy as jnp
from jax import lax
from jax.experimental import pallas as pl
from jax.experimental.pallas import tpu as pltpu
from jax.sharding import PartitionSpec as P

F32 = jnp.float32
BF16 = jnp.bfloat16
BATCH = 8
EMBED = 512
TILE = 256
DEVS = 64


class Tower:
    def __init__(self, width, heads, hidden, length, padded, rows, causal):
        self.width = width
        self.heads = heads
        self.hidden = hidden
        self.length = length
        self.padded = padded
        self.real = BATCH * length
        self.rows = rows
        self.spread = BATCH * padded
        self.causal = causal


IMAGE = Tower(768, 12, 3072, 50, 64, 400, False)
TEXT = Tower(512, 8, 2048, 77, 80, 640, True)

VMEM_LIMIT = 58 * 1024 * 1024


def mm(left, right):
    return lax.dot_general(left, right, (((1,), (0,)), ((), ())), preferred_element_type=F32)


def mm_nt(left, right):
    return lax.dot_general(left, right, (((1,), (1,)), ((), ())), preferred_element_type=F32)


def mm_tn(left, right):
    return lax.dot_general(left, right, (((0,), (0,)), ((), ())), preferred_element_type=F32)


def normalise(values):
    centre = jnp.mean(values, axis=-1, keepdims=True)
    offset = values - centre
    inverse = lax.rsqrt(jnp.mean(offset * offset, axis=-1, keepdims=True) + 1e-05)
    return offset * inverse, inverse


def norm_back(upstream, gain, normal, inverse):
    scaled = upstream * gain
    inner = (
        scaled
        - jnp.mean(scaled, axis=-1, keepdims=True)
        - normal * jnp.mean(scaled * normal, axis=-1, keepdims=True)
    )
    return inner * inverse


def column_sum(values):
    return jnp.sum(values, axis=0, keepdims=True)


def sigmoid(values):
    return 1.0 / (1.0 + jnp.exp(-values))


def vec(ref):
    return ref[...].reshape(1, -1)


def chunks(count, size=128):
    return [(at, min(size, count - at)) for at in range(0, count, size)]


def loop(count, body):
    def step(i, carry):
        body(i)
        return carry

    lax.fori_loop(0, count, step, 0)


def tile_loop(width, body):
    loop(width // TILE, lambda n: body(n, pl.ds(pl.multiple_of(n * TILE, TILE), TILE)))


def put_tiles(ref, n, rows, values):
    for i in range(TILE // 128):
        ref[n * (TILE // 128) + i, 0:rows, :] = values[:, 128 * i : 128 * i + 128]


def head_masks():
    lane = lax.broadcasted_iota(jnp.int32, (1, 128), 1)
    first = jnp.where(lane < 64, 1.0, 0.0).astype(BF16)
    second = jnp.where(lane < 64, 0.0, 1.0).astype(BF16)
    return first, second


def two_heads(values, masks):
    return jnp.concatenate([values * masks[0], values * masks[1]], axis=0)


def own_head(values, padded):
    lane = lax.broadcasted_iota(jnp.int32, (padded, 128), 1)
    return jnp.where(lane < 64, values[:padded], values[padded:])


def pooled_row(t, ends, b):
    return ends[b] * BATCH + b


def front_kernel(
    t,
    ends,
    tokens,
    first_gain,
    first_shift,
    joint_weight,
    output_weight,
    second_gain,
    second_shift,
    widen_weight,
    narrow_weight,
    final_gain,
    final_shift,
    projection,
    normed_one,
    joint,
    probs,
    context,
    mixed,
    mixed_row,
    wide_row,
    pooled,
    raw_out,
    unit,
    joint_wide,
    context_wide,
):
    width, padded, rows = t.width, t.padded, t.rows
    if t.real < rows:
        normed_one[t.real - 8 : rows, :] = jnp.zeros((rows - t.real + 8, width), BF16)
    for at, size in chunks(t.real):
        normal, _ = normalise(tokens[at : at + size, :].astype(F32))
        normed_one[at : at + size, :] = (normal * vec(first_gain) + vec(first_shift)).astype(BF16)
    if t.spread > rows:
        fill = (3 * width // 128, t.spread - rows, 128)
        joint_wide[:, rows : t.spread, :] = jnp.zeros(fill, F32)

    def joint_step(n, cols):
        put_tiles(joint_wide, n, rows, mm(normed_one[...], joint_weight[:, cols]))

    tile_loop(3 * width, joint_step)

    masks = head_masks()
    key_at = lax.broadcasted_iota(jnp.int32, (padded, 2 * padded), 0)
    query_at = lax.broadcasted_iota(jnp.int32, (padded, 2 * padded), 1)
    query_at = jnp.where(query_at < padded, query_at, query_at - padded)
    valid = key_at <= query_at if t.causal else key_at < t.length
    pairs = range(t.heads // 2)

    def attend(b):
        some = pl.ds(b, padded, stride=BATCH)
        for c in range(3 * width // 128):
            joint[b, :, 128 * c : 128 * c + 128] = joint_wide[c, some, :].astype(BF16)
        scores = []
        for p in pairs:
            at = 128 * p
            queries = joint[b, :, at : at + 128]
            keys = joint[b, :, width + at : width + at + 128]
            scores.append(mm_nt(keys, two_heads(queries, masks)) * 0.125)
        lows = []
        for p in pairs:
            score = jnp.where(valid, scores[p], -1e30)
            raised = jnp.exp(score - jnp.max(score, axis=0, keepdims=True))
            low = (raised * (1.0 / column_sum(raised))).astype(BF16)
            probs[b, p] = low
            lows.append(low)
        for p in pairs:
            at = 2 * width + 128 * p
            both = mm_tn(lows[p], joint[b, :, at : at + 128])
            context_wide[p, some, :] = own_head(both, padded)

    loop(BATCH, attend)
    for p in pairs:
        context[:, 128 * p : 128 * p + 128] = context_wide[p, 0:rows, :].astype(BF16)

    def mix_step(n, cols):
        mixed[:, cols] = mm(context[...], output_weight[:, cols])

    tile_loop(width, mix_step)
    for at, size in chunks(t.real):
        mixed[at : at + size, :] += tokens[at : at + size, :].astype(F32)
    for b in range(BATCH):
        mixed_row[b : b + 1, :] = mixed[pl.ds(pooled_row(t, ends, b), 1), :]

    row = mixed_row[...]
    normal, _ = normalise(row)
    normed = (normal * vec(second_gain) + vec(second_shift)).astype(BF16)
    wide = mm(normed, widen_weight[...])
    wide_row[...] = wide
    active = (wide * sigmoid(1.702 * wide)).astype(BF16)
    last = row + mm(active, narrow_weight[...])
    pooled[...] = last
    normal, _ = normalise(last)
    normed = (normal * vec(final_gain) + vec(final_shift)).astype(BF16)
    raw = mm(normed, projection[...])
    raw_out[...] = raw
    factor = lax.rsqrt(jnp.sum(raw * raw, axis=-1, keepdims=True) + 1e-06)
    unit[...] = (raw * factor).astype(BF16)


def middle_kernel(
    t,
    ends,
    mixed,
    block_grad,
    second_gain,
    second_shift,
    widen_weight,
    narrow_weight,
    normed_two,
    active_out,
    widened_grad,
    mixed_grad,
    grad_row,
    gain_grad,
    shift_grad,
    narrow_in,
    wide_in,
):
    step = pl.program_id(0)

    @pl.when(step == 0)
    def _():
        if t.real < t.rows:
            wide_in[t.real : t.rows, :] = jnp.zeros((t.rows - t.real, t.width), F32)
        for at, size in chunks(t.rows):
            normal, _ = normalise(mixed[at : at + size, :])
            normed_two[at : at + size, :] = (normal * vec(second_gain) + vec(second_shift)).astype(
                BF16
            )
        for at, size in chunks(t.real):
            wide_in[at : at + size, :] = block_grad[at : at + size, :].astype(F32)
        for b in range(BATCH):
            row = pl.ds(pooled_row(t, ends, b), 1)
            grad_row[b : b + 1, :] = wide_in[row, :]
            wide_in[row, :] = jnp.zeros((1, t.width), F32)
        narrow_in[...] = wide_in[...].astype(BF16)
        mixed_grad[...] = jnp.zeros_like(mixed_grad)

    wide = mm(normed_two[...], widen_weight[...])
    sig = sigmoid(1.702 * wide)
    active_out[...] = (wide * sig).astype(BF16)
    slope = sig + 1.702 * wide * sig * (1.0 - sig)
    low = (mm_nt(narrow_in[...], narrow_weight[...]) * slope).astype(BF16)
    widened_grad[...] = low
    mixed_grad[...] += mm_nt(low, widen_weight[...])

    @pl.when(step == pl.num_programs(0) - 1)
    def _():
        gain = shift = 0.0
        for at, size in chunks(t.rows):
            some = slice(at, at + size)
            normal, inverse = normalise(mixed[some, :])
            up = mixed_grad[some, :]
            gain += column_sum(up * normal)
            shift += column_sum(up)
            mixed_grad[some, :] = wide_in[some, :] + norm_back(
                up, vec(second_gain), normal, inverse
            )
        gain_grad[...] = gain
        shift_grad[...] = shift


def split_dot(weights, right):
    high = weights.astype(BF16)
    rest = weights - high.astype(F32)
    middle = rest.astype(BF16)
    low = (rest - middle.astype(F32)).astype(BF16)
    return mm(high, right) + mm(middle, right) + mm(low, right)


def head_back(
    unit_grad,
    raw,
    pooled,
    mixed_row,
    wide_row,
    grad_row,
    final_gain,
    final_shift,
    second_gain,
    second_shift,
    projection,
    widen_weight,
    narrow_weight,
    outs,
):
    (
        final_gain_grad,
        final_shift_grad,
        second_gain_grad,
        second_shift_grad,
        final_out,
        raw_grad_out,
        narrow_in_row,
        wide_grad_row,
        mixed_grad_row,
    ) = outs
    factor = lax.rsqrt(jnp.sum(raw * raw, axis=-1, keepdims=True) + 1e-06)
    raw_grad = factor * unit_grad - raw * (factor * factor * factor) * jnp.sum(
        unit_grad * raw, axis=-1, keepdims=True
    )
    raw_grad = raw_grad.astype(BF16)
    raw_grad_out[...] = raw_grad.astype(F32)
    normal, inverse = normalise(pooled)
    final_out[...] = (normal * final_gain + final_shift).astype(BF16).astype(F32)
    up = mm_nt(raw_grad, projection[...])
    final_gain_grad[...] = column_sum(up * normal)
    final_shift_grad[...] = column_sum(up)
    out_grad = grad_row + norm_back(up, final_gain, normal, inverse)
    narrow_in = out_grad.astype(BF16)
    narrow_in_row[...] = narrow_in.astype(F32)
    sig = sigmoid(1.702 * wide_row)
    slope = sig + 1.702 * wide_row * sig * (1.0 - sig)
    low = (mm_nt(narrow_in, narrow_weight[...]) * slope).astype(BF16)
    wide_grad_row[...] = low.astype(F32)
    up = mm_nt(low, widen_weight[...])
    normal, inverse = normalise(mixed_row)
    second_gain_grad[...] = column_sum(up * normal)
    second_shift_grad[...] = column_sum(up)
    mixed_grad_row[...] = out_grad + norm_back(up, second_gain, normal, inverse)


def pair_kernel(place, log_scale, own, other, image_unit, text_unit, *refs):
    image_in, text_in = refs[:12], refs[12:24]
    loss, scale_grad = refs[24], refs[25]
    image_outs, text_outs = refs[26:35], refs[35:44]
    half = own.shape[0]
    pairs = 2 * half
    scale = jnp.exp(jnp.full((1, 1), log_scale[0], F32))
    blocks = (own, other)

    def totals(left_at, right_at):
        sums, moments = [], []
        for right in blocks:
            column, moment = None, None
            for left in blocks:
                for piece in range(0, half, 256):
                    sims = scale * mm_nt(
                        left[piece : piece + 256, left_at : left_at + EMBED],
                        right[:, right_at : right_at + EMBED],
                    )
                    raised = jnp.exp(sims)
                    add, more = column_sum(raised), column_sum(raised * sims)
                    column = add if column is None else column + add
                    moment = more if moment is None else moment + more
            sums.append(column)
            moments.append(moment)
        return sums, moments

    column_sums, column_moments = totals(0, EMBED)
    row_sums, row_moments = totals(EMBED, 0)
    log_total = jnp.zeros((1, 1), F32)
    weighted = jnp.zeros((1, 1), F32)
    trace = jnp.zeros((1, 1), F32)
    for i in range(2):
        for total, moment in ((column_sums[i], column_moments[i]), (row_sums[i], row_moments[i])):
            log_total += jnp.sum(jnp.log(total), axis=-1, keepdims=True)
            weighted += jnp.sum(moment / total, axis=-1, keepdims=True)
        product = blocks[i][:, :EMBED].astype(F32) * blocks[i][:, EMBED:].astype(F32)
        trace += jnp.sum(column_sum(product), axis=-1, keepdims=True)
    trace = scale * trace
    loss[...] = jnp.broadcast_to((log_total - 2.0 * trace) / (2.0 * pairs), loss.shape)
    scale_grad[...] = jnp.broadcast_to((weighted - 2.0 * trace) / (2.0 * pairs), loss.shape)

    lane = lax.broadcasted_iota(jnp.int32, (BATCH, half), 1)
    sub = lax.broadcasted_iota(jnp.int32, (BATCH, half), 0)
    identity = jnp.where(lane == sub + place[1] * BATCH, 2.0, 0.0)

    def grads(unit, at, other_sums):
        raised = [jnp.exp(scale * mm_nt(unit[...], block[:, at : at + EMBED])) for block in blocks]
        own_sum = sum(jnp.sum(r, axis=-1, keepdims=True) for r in raised)
        result = None
        for i in range(2):
            weight = raised[i] * (1.0 / own_sum + 1.0 / other_sums[i])
            if i == 0:
                weight = weight - identity
            weight = weight / (2.0 * pairs)
            part = split_dot(weight, blocks[i][:, at : at + EMBED])
            result = part if result is None else result + part
        return scale * result

    image_grad = grads(image_unit, EMBED, column_sums)
    text_grad = grads(text_unit, 0, row_sums)
    for unit_grad, ins, outs in (
        (image_grad, image_in, image_outs),
        (text_grad, text_in, text_outs),
    ):
        values = [ref[...] for ref in ins[:5]] + [vec(ref) for ref in ins[5:9]]
        head_back(unit_grad, *values, *ins[9:12], outs)


def back_kernel(
    t,
    ends,
    mixed_grad,
    mixed_grad_row,
    joint,
    probs,
    tokens,
    first_gain,
    output_weight,
    joint_weight,
    grads,
    tokens_grad,
    gain_grad,
    shift_grad,
    grad,
    context_grad,
    joint_grad,
    normed_grad,
):
    width, padded, rows = t.width, t.padded, t.rows
    grad[...] = mixed_grad[...]
    for b in range(BATCH):
        grad[pl.ds(pooled_row(t, ends, b), 1), :] = mixed_grad_row[b : b + 1, :]
    mixed_low = slice(3 * width, 4 * width)
    grads[:, mixed_low] = grad[...].astype(BF16)
    if t.spread > rows:
        fill = (width // 128, t.spread - rows, 128)
        context_grad[:, rows : t.spread, :] = jnp.zeros(fill, F32)

    def context_step(n, cols):
        put_tiles(context_grad, n, rows, mm_nt(grads[:, mixed_low], output_weight[cols, :]))

    tile_loop(width, context_step)
    masks = head_masks()
    pairs = range(t.heads // 2)

    def attend(b):
        some = pl.ds(b, padded, stride=BATCH)
        ups = [two_heads(context_grad[p, some, :].astype(BF16), masks) for p in pairs]
        backs = []
        for p in pairs:
            at = 2 * width + 128 * p
            backs.append(mm_nt(joint[b, :, at : at + 128], ups[p]))
        lows = []
        for p in pairs:
            wide = probs[b, p].astype(F32)
            back = wide * (backs[p] - column_sum(backs[p] * wide))
            lows.append(back.astype(BF16))
        for p in pairs:
            at = 128 * p
            queries = joint[b, :, at : at + 128]
            keys = joint[b, :, width + at : width + at + 128]
            joint_grad[2 * len(pairs) + p, some, :] = mm(probs[b, p], ups[p])
            joint_grad[len(pairs) + p, some, :] = mm(lows[p], two_heads(queries, masks)) * 0.125
            joint_grad[p, some, :] = own_head(mm_tn(lows[p], keys), padded) * 0.125

    loop(BATCH, attend)
    for c in range(3 * width // 128):
        grads[:, 128 * c : 128 * c + 128] = joint_grad[c, 0:rows, :].astype(BF16)

    def normed_step(n, cols):
        normed_grad[:, cols] = mm_nt(grads[:, 0 : 3 * width], joint_weight[cols, :])

    tile_loop(width, normed_step)
    gain = shift = 0.0
    for at, size in chunks(t.real):
        some = slice(at, at + size)
        normal, inverse = normalise(tokens[some, :].astype(F32))
        up = normed_grad[some, :]
        gain += column_sum(up * normal)
        shift += column_sum(up)
        tokens_grad[some, :] = grad[some, :] + norm_back(up, vec(first_gain), normal, inverse)
    gain_grad[...] = gain
    shift_grad[...] = shift


def turn(source, target):
    def step(n):
        cols = pl.ds(pl.multiple_of(n * 128, 128), 128)
        target[cols, :] = source[:, cols].T

    loop(source.shape[1] // 128, step)


def lanes_down(values):
    return jnp.concatenate(
        [values[:, :, at : at + 128] for at in range(0, values.shape[2], 128)], axis=1
    )


def put(out, received, devices, units, values):
    count = values.shape[1] // 16
    values = values.reshape(values.shape[0], count, 16, 128)
    if received is not None:
        values = values + received[devices, units : units + count].astype(F32)
    out[devices, units : units + count] = values.astype(BF16)


def pack_twelve(first, second, received, out, unit=0, each=4):
    cols = first.shape[1]
    count = cols // 128
    sub = lax.broadcasted_iota(jnp.int32, (each, 8, cols), 1) < 4

    def step(e):
        rows = pl.ds(pl.multiple_of(e * (24 * each), 8), 24 * each)
        x = first[rows, :].reshape(each, 24, cols)
        y = second[rows, :].reshape(each, 24, cols)
        left, right = x[:, 8:16], y[:, 8:16]
        even = jnp.where(sub, left, pltpu.roll(right, 4, 1))
        odd = jnp.where(sub, pltpu.roll(left, 4, 1), right)
        parts = []
        for a, b, c in ((x[:, 0:8], y[:, 0:8], even), (x[:, 16:24], y[:, 16:24], odd)):
            parts.append(jnp.concatenate([lanes_down(v) for v in (a, b, c)], axis=1))
        if parts[0].shape[1] % 16:
            fill = jnp.zeros((each, 16 - parts[0].shape[1] % 16, 128), F32)
            parts = [jnp.concatenate([part, fill], axis=1) for part in parts]
        height = parts[0].shape[1]
        values = jnp.stack(parts, axis=1).reshape(2 * each, height, 128)
        devices = pl.ds(pl.multiple_of(e * (2 * each), 2 * each), 2 * each)
        put(out, received, devices, unit, values)

    loop(32 // each, step)


def pack_rows(result, rows, received, out, unit=0, each=8):
    total = result.shape[0] // rows
    cols = result.shape[1]

    def step(e):
        some = pl.ds(pl.multiple_of(e * (rows * each), 8), rows * each)
        values = lanes_down(result[some, :].reshape(each, rows, cols))
        put(out, received, pl.ds(pl.multiple_of(e * each, each), each), unit, values)

    loop(total // each, step)


def take_patched(t, ends, source, new, target):
    real = source.shape[0]
    if real < t.rows:
        target[real - 8 :, :] = jnp.zeros((t.rows - real + 8, target.shape[1]), BF16)
    target[0:real, :] = source[...]
    sub = lax.broadcasted_iota(jnp.int32, (16, 1), 0)

    def patch(b):
        row = pooled_row(t, ends, b)
        base = pl.multiple_of((row // 16) * 16, 16)
        some = pl.ds(base, 16)
        old = target[some, :].astype(F32)
        target[some, :] = jnp.where(sub == row - base, new[pl.ds(b, 1), :], old).astype(BF16)

    loop(BATCH, patch)


def wide_weight_kernel(t, patched, added, buffered, left_count, place, ends, *refs):
    refs = list(refs)
    lefts = [refs.pop(0) for _ in range(left_count)]
    tiles = [refs.pop(0) for _ in range(2 if t is IMAGE else 1)]
    news = [refs.pop(0) for _ in tiles] if patched else [None] * len(tiles)
    received = refs.pop(0) if added else None
    if buffered:
        refs.pop(0)
    out = refs.pop(0)
    turned = [refs.pop(0) for _ in range(left_count)]
    results = [refs.pop(0) for _ in tiles]
    step = pl.program_id(0)

    @pl.when(step == 0)
    def _():
        for left, target in zip(lefts, turned):
            turn(left, target)

    half = place[0] if added else 1 - place[0]
    for i, (tile, new, result) in enumerate(zip(tiles, news, results)):
        if patched:
            ready = refs[i]
            take_patched(t, ends, tile, new, ready)
            tile = ready
        if left_count == 1:
            result[...] = mm(turned[0][...], tile[...])
        else:
            steps = pl.num_programs(0)
            at = half * (len(tiles) * steps) + i * steps + step
            late = at >= 3 * t.width // tile.shape[1]

            @pl.when(late)
            def _():
                result[...] = mm(turned[1][...], tile[...])

            @pl.when(jnp.logical_not(late))
            def _():
                result[...] = mm(turned[0][...], tile[...])

    if t is IMAGE:
        pack_twelve(*results, received, out)
    else:
        pack_rows(results[0], 8, received, out)


def narrow_weight_kernel(t, added, place, ends, active, grad, new, *refs):
    refs = list(refs)
    received = refs.pop(0) if added else None
    refs.pop(0)
    out, turned, result, ready = refs
    step = pl.program_id(0)

    @pl.when(step == 0)
    def _():
        take_patched(t, ends, grad, new, ready)

    turn(active, turned)
    result[...] = mm(turned[...], ready[...])
    pack_rows(result, t.hidden // DEVS, received, out, each=4)


FEED_UNITS = 27
REST_UNITS = 18
FEED_AT = {"text": (0, 4), "image": (9, 18)}
REST_AT = {"text": 0, "image": 9}
MISC_AT = 4


def buffer_call(kernel, name, grid, scalars, ins, units, block, at, scratch, flops, added, received, buffer):
    def where(i, *_):
        if block[0] == DEVS:
            return (0, at // block[1] + i, 0, 0)
        return (i, at // block[1], 0, 0)

    spec = pl.BlockSpec((block[0], block[1], 16, 128), where)
    arrays = [a for a, _ in ins]
    specs = [s for _, s in ins]
    if added:
        arrays.append(received)
        specs.append(spec)
    aliases = {}
    if buffer is not None:
        aliases = {len(scalars) + len(arrays): 0}
        arrays.append(buffer)
        specs.append(pl.BlockSpec(memory_space=pl.ANY))
    return pl.pallas_call(
        kernel,
        name=name,
        out_shape=jax.ShapeDtypeStruct((DEVS, units, 16, 128), BF16),
        grid_spec=pltpu.PrefetchScalarGridSpec(
            num_scalar_prefetch=len(scalars),
            grid=(grid,),
            in_specs=specs,
            out_specs=spec,
            scratch_shapes=[pltpu.VMEM(shape, kind) for shape, kind in scratch],
        ),
        input_output_aliases=aliases,
        compiler_params=pltpu.CompilerParams(vmem_limit_bytes=VMEM_LIMIT),
        cost_estimate=pl.CostEstimate(flops=flops, bytes_accessed=8 << 20, transcendentals=0),
    )(*scalars, *arrays)


def whole(array):
    return array, pl.BlockSpec(array.shape, lambda i, *_: (0,) * array.ndim)


def wide_weights(t, name, place, ends, lefts, grad, new, units, at, received, buffer):
    added = received is not None
    steps = 3 if t is IMAGE else 2
    cols = TILE if t is IMAGE else 512

    def columns(shift):
        def index(i, place, ends):
            half = place[0] if added else 1 - place[0]
            return (0, half * (2 * steps if t is IMAGE else steps) + shift + i)

        return index

    shifts = (0, steps) if t is IMAGE else (0,)
    ins = [whole(left) for left in lefts]
    ins += [(grad, pl.BlockSpec((t.rows, cols), columns(s))) for s in shifts]
    if new is not None:
        ins += [(new, pl.BlockSpec((BATCH, cols), columns(s))) for s in shifts]
    scratch = [((t.width, t.rows), BF16) for _ in lefts]
    scratch += [((t.width, cols), F32) for _ in shifts]
    if new is not None:
        scratch += [((t.rows, cols), BF16) for _ in shifts]
    kernel = functools.partial(
        wide_weight_kernel, t, new is not None, added, buffer is not None, len(lefts)
    )
    block = (DEVS, 3 if t is IMAGE else 2)
    flops = 4 * t.rows * t.width * t.width * 2
    return buffer_call(
        kernel, name, steps, (place, ends), ins, units, block, at, scratch, flops, added, received, buffer
    )


def narrow_weights(t, name, place, ends, active, grad, new, units, at, received, buffer):
    added = received is not None
    cols = t.width // 2

    def column(i, place, ends):
        return (0, place[0] if added else 1 - place[0])

    ins = [
        (active, pl.BlockSpec((t.rows, t.width), lambda i, *_: (0, i))),
        (grad, pl.BlockSpec((t.real, cols), column)),
        (new, pl.BlockSpec((BATCH, cols), column)),
    ]
    scratch = [((t.width, t.rows), BF16), ((t.width, cols), F32), ((t.rows, cols), BF16)]
    block = (16, 9 if t is IMAGE else 4)
    flops = 4 * t.rows * t.width * t.width * 2
    return buffer_call(
        functools.partial(narrow_weight_kernel, t, added),
        name,
        4,
        (place, ends),
        ins,
        units,
        block,
        at,
        scratch,
        flops,
        added,
        received,
        buffer,
    )


def misc_kernel(added, place, *refs):
    refs = list(refs)
    image_final, image_raw, text_final, text_raw = refs[:4]
    refs = refs[4:]
    half = place[0] if added else 1 - place[0]
    received = None
    if added:
        vectors, received, refs = refs[:16], refs[16], refs[17:]
    _, out, first, second, third = refs[:5]

    def columns(ref, at, size):
        return ref[:, pl.ds(pl.multiple_of(half * 256 + at, 128), size)].astype(BF16)

    final = image_final[...].astype(BF16)
    first[...] = mm_tn(final, columns(image_raw, 0, 128))
    second[...] = mm_tn(final, columns(image_raw, 128, 128))
    pack_twelve(first, second, received, out, 2, 8)
    third[...] = mm_tn(text_final[...].astype(BF16), columns(text_raw, 0, 256))
    pack_rows(third, 8, received, out, 0)
    if not added:
        out[:, 1] = jnp.zeros((DEVS, 16, 128), BF16)
        return
    spread = refs[5]
    spread[...] = jnp.zeros_like(spread)
    for tower, refs_of, width in ((0, vectors[:8], 768), (1, vectors[8:], 512)):
        each = width // DEVS
        device = lax.broadcasted_iota(jnp.int32, (DEVS, width), 0)
        column = lax.broadcasted_iota(jnp.int32, (DEVS, width), 1)
        mine = jnp.logical_and(column >= device * each, column < device * each + each)
        source = lax.broadcasted_iota(jnp.int32, (width, 128), 0)
        lane = lax.broadcasted_iota(jnp.int32, (width, 128), 1)
        at = lax.rem(source, each)
        high_at = jnp.where(lane == at, 1.0, 0.0).astype(BF16)
        low_at = jnp.where(lane == at + 64, 1.0, 0.0).astype(BF16)
        rows = [refs_of[0][...], refs_of[1][...], refs_of[2][...] + refs_of[3][...]]
        rows += [refs_of[4][...] + refs_of[5][...], refs_of[6][...], refs_of[7][...]]
        for k, row in enumerate(rows):
            row = jnp.where(mine, row, 0.0)
            high = row.astype(BF16)
            low = (row - high.astype(F32)).astype(BF16)
            spread[:, 6 * tower + k, :] = mm(high, high_at) + mm(low, low_at)
    out[:, 1] = spread[...].astype(BF16)


def misc(place, heads, vectors, received, buffer):
    added = received is not None
    ins = [whole(a) for a in (heads[0][4], heads[0][5], heads[1][4], heads[1][5])]
    if added:
        ins += [whole(v) for v in vectors]
    scratch = [((768, 128), F32), ((768, 128), F32), ((512, 256), F32)]
    if added:
        scratch.append(((DEVS, 16, 128), F32))
    return buffer_call(
        functools.partial(misc_kernel, added),
        "misc",
        1,
        (place,),
        ins,
        REST_UNITS,
        (DEVS, 4),
        MISC_AT,
        scratch,
        1 << 28,
        added,
        received,
        buffer,
    )


def add_kernel(received, total):
    total[...] = jnp.sum(received[...].astype(F32), axis=0)


def sum_blocks(received, block):
    count, units = received.shape[:2]
    return pl.pallas_call(
        add_kernel,
        name="sum_blocks",
        grid=(units // block,),
        out_shape=jax.ShapeDtypeStruct((units, 16, 128), F32),
        in_specs=[pl.BlockSpec((count, block, 16, 128), lambda i: (0, i, 0, 0))],
        out_specs=pl.BlockSpec((block, 16, 128), lambda i: (i, 0, 0)),
        compiler_params=pltpu.CompilerParams(vmem_limit_bytes=VMEM_LIMIT),
    )(received)


def unpack_kernel(place, feed_mine, rest_mine, feed_other, rest_other, *outs):
    (
        image_joint,
        image_output,
        image_widen,
        image_narrow,
        image_projection,
        text_joint,
        text_output,
        text_widen,
        text_narrow,
        text_projection,
    ) = outs[:10]
    odd = place[1] % 2

    def emit(half, feed, rest):
        def into(ref, col, body, tail):
            @pl.when(odd == 0)
            def _():
                ref[0:8, col : col + 128] = body
                ref[8:12, col : col + 128] = tail

            @pl.when(odd == 1)
            def _():
                ref[0:4, col : col + 128] = tail
                ref[4:12, col : col + 128] = body

        def image_wide(source, at, store):
            for tile in range(3):
                block = source[16 * (at + 3 * tile) : 16 * (at + 3 * tile) + 48, :]
                for side in range(2):
                    for g in range(2):
                        body = block[16 * side + 8 * g : 16 * side + 8 * g + 8]
                        tail = block[32 + 8 * g + 4 * side : 36 + 8 * g + 4 * side]
                        store(half * 1536 + side * 768 + tile * 256 + g * 128, body, tail)

        def joint_store(col, body, tail):
            if col < 2304:
                into(image_joint, col, body, tail)
            else:
                into(image_output, col - 2304, body, tail)

        image_wide(feed, FEED_AT["image"][0], functools.partial(into, image_widen))
        image_wide(rest, REST_AT["image"], joint_store)
        at = 16 * FEED_AT["image"][1]
        for g in range(3):
            col = half * 384 + 128 * g
            image_narrow[:, col : col + 128] = feed[at + 48 * g : at + 48 * g + 48, :]
        at = 16 * (MISC_AT + 2)
        for side in range(2):
            col = half * 256 + 128 * side
            tail = rest[at + 16 + 4 * side : at + 20 + 4 * side, :]
            into(image_projection, col, rest[at + 8 * side : at + 8 * side + 8, :], tail)
        for g in range(8):
            col = half * 1024 + 128 * g
            text_widen[:, col : col + 128] = feed[8 * g : 8 * g + 8, :]
            block = rest[8 * g : 8 * g + 8, :]
            if col < 1536:
                text_joint[:, col : col + 128] = block
            else:
                text_output[:, col - 1536 : col - 1408] = block
        for g in range(2):
            col = half * 256 + 128 * g
            text_narrow[:, col : col + 128] = feed[64 + 32 * g : 96 + 32 * g, :]
            at = 16 * MISC_AT + 8 * g
            text_projection[:, col : col + 128] = rest[at : at + 8, :]

    for half in range(2):

        @pl.when(place[0] == half)
        def _():
            emit(half, feed_mine, rest_mine)
            emit(1 - half, feed_other, rest_other)

    at = 16 * (MISC_AT + 1)
    vectors = rest_mine[at : at + 16, :] + rest_other[at : at + 16, :]
    for k in range(12):
        each = 12 if k < 6 else 8
        outs[10 + k][...] = vectors[k : k + 1, 0:each] + vectors[k : k + 1, 64 : 64 + each]


SMEM = pl.BlockSpec(memory_space=pltpu.SMEM)
VMEM = pl.BlockSpec(memory_space=pltpu.VMEM)


def call(body, name, scalars, arrays, outs, scratch=(), flops=1 << 32):
    return pl.pallas_call(
        body,
        name=name,
        out_shape=tuple(jax.ShapeDtypeStruct(shape, kind) for shape, kind in outs),
        in_specs=[SMEM] * len(scalars) + [VMEM] * len(arrays),
        out_specs=tuple(VMEM for _ in outs),
        scratch_shapes=[pltpu.VMEM(shape, kind) for shape, kind in scratch],
        compiler_params=pltpu.CompilerParams(vmem_limit_bytes=VMEM_LIMIT),
        cost_estimate=pl.CostEstimate(flops=flops, bytes_accessed=20 << 20, transcendentals=0),
    )(*scalars, *arrays)


def front(t, name, ends, tokens, params):
    rows, width, hidden = t.rows, t.width, t.hidden
    return call(
        functools.partial(front_kernel, t),
        name + "_front",
        (ends,),
        (tokens, *params),
        (
            ((rows, width), BF16),
            ((BATCH, t.padded, 3 * width), BF16),
            ((BATCH, t.heads // 2, t.padded, 2 * t.padded), BF16),
            ((rows, width), BF16),
            ((rows, width), F32),
            ((BATCH, width), F32),
            ((BATCH, hidden), F32),
            ((BATCH, width), F32),
            ((BATCH, EMBED), F32),
            ((BATCH, EMBED), BF16),
        ),
        (((3 * width // 128, t.spread, 128), F32), ((width // 128, t.spread, 128), F32)),
    )


def middle(t, name, ends, mixed, block_grad, gain, shift, widen, narrow):
    rows, width, hidden = t.rows, t.width, t.hidden
    outs = (
        ((rows, width), BF16),
        ((rows, hidden), BF16),
        ((rows, hidden), BF16),
        ((rows, width), F32),
        ((BATCH, width), F32),
        ((1, width), F32),
        ((1, width), F32),
    )

    def held(shape):
        return pl.BlockSpec(shape, lambda i, *_: (0,) * len(shape))

    tiled = pl.BlockSpec((rows, TILE), lambda i, *_: (0, i))
    out_specs = [held(shape) for shape, _ in outs]
    out_specs[1] = out_specs[2] = tiled
    in_specs = [held(a.shape) for a in (mixed, block_grad, gain, shift)]
    in_specs.append(pl.BlockSpec((width, TILE), lambda i, *_: (0, i)))
    in_specs.append(pl.BlockSpec((TILE, width), lambda i, *_: (i, 0)))
    return pl.pallas_call(
        functools.partial(middle_kernel, t),
        name=name + "_middle",
        out_shape=tuple(jax.ShapeDtypeStruct(shape, kind) for shape, kind in outs),
        grid_spec=pltpu.PrefetchScalarGridSpec(
            num_scalar_prefetch=1,
            grid=(hidden // TILE,),
            in_specs=in_specs,
            out_specs=tuple(out_specs),
            scratch_shapes=[pltpu.VMEM((rows, width), BF16), pltpu.VMEM((rows, width), F32)],
        ),
        compiler_params=pltpu.CompilerParams(vmem_limit_bytes=VMEM_LIMIT),
        cost_estimate=pl.CostEstimate(flops=1 << 33, bytes_accessed=20 << 20, transcendentals=0),
    )(ends, mixed, block_grad, gain, shift, widen, narrow)


def back(t, name, ends, mixed_grad, row, joint, probs, tokens, gain, output, joint_weight):
    rows, width = t.rows, t.width
    return call(
        functools.partial(back_kernel, t),
        name + "_back",
        (ends,),
        (mixed_grad, row, joint, probs, tokens, gain, output, joint_weight),
        (
            ((rows, 4 * width), BF16),
            ((t.real, width), F32),
            ((1, width), F32),
            ((1, width), F32),
        ),
        (
            ((rows, width), F32),
            ((width // 128, t.spread, 128), F32),
            ((3 * width // 128, t.spread, 128), F32),
            ((rows, width), F32),
        ),
        1 << 33,
    )


SWAP = [(0, 1), (1, 0)]


def by_token(tokens):
    return tokens.transpose(1, 0, 2).reshape(-1, tokens.shape[2])


def shards(*args):
    image_tokens, image_weights, image_block_grad = args[0], args[1:12], args[12]
    text_tokens, caption_lengths = args[13], args[14]
    text_weights, text_block_grad, log_scale = args[15:26], args[26], args[27]
    core = lax.axis_index("tower")
    dp = lax.axis_index("dp")
    place = jnp.stack([core, dp]).astype(jnp.int32)
    image_ends = jnp.zeros((BATCH,), jnp.int32)
    text_ends = (caption_lengths - 1).astype(jnp.int32)
    towers = (
        (IMAGE, "image", image_ends, by_token(image_tokens), image_weights, by_token(image_block_grad)),
        (TEXT, "text", text_ends, by_token(text_tokens), text_weights, by_token(text_block_grad)),
    )
    fronts = [front(t, name, ends, tokens, w) for t, name, ends, tokens, w, _ in towers]
    units = [f[9] for f in fronts]
    both = jnp.concatenate(units, axis=1)
    own = lax.all_to_all(
        jnp.broadcast_to(both[None], (DEVS, *both.shape)), "dp", 0, 0, tiled=True
    ).reshape(DEVS * BATCH, 2 * EMBED)
    other = lax.ppermute(own, "tower", SWAP)

    middles = []
    for (t, name, ends, _, w, block_grad), f in zip(towers, fronts):
        middles.append(middle(t, name, ends, f[4], block_grad, w[4], w[5], w[6], w[7]))

    pair_in = []
    pair_out = [((1, 128), F32), ((1, 128), F32)]
    for (t, _, _, _, w, _), f, m in zip(towers, fronts, middles):
        pair_in += [f[8], f[7], f[5], f[6], m[4], w[8], w[9], w[4], w[5], w[10], w[6], w[7]]
        pair_out += [((1, t.width), F32)] * 4 + [
            ((BATCH, t.width), F32),
            ((BATCH, EMBED), F32),
            ((BATCH, t.width), F32),
            ((BATCH, t.hidden), F32),
            ((BATCH, t.width), F32),
        ]
    paired = call(
        pair_kernel, "pairs", (place, log_scale), (own, other, *units, *pair_in), pair_out
    )
    loss, scale_grad = paired[0][0, :1], paired[1][0, :1]
    heads = (paired[2:11], paired[11:20])

    def feed(received):
        buffer = None
        for (t, name, ends, _, _, block_grad), m, h in zip(towers, middles, heads):
            at = FEED_AT[name]
            buffer = wide_weights(
                t, name + "_widen", place, ends, (m[0],), m[2], h[7], FEED_UNITS, at[0], received, buffer
            )
            buffer = narrow_weights(
                t, name + "_narrow", place, ends, m[1], block_grad, h[6], FEED_UNITS, at[1], received, buffer
            )
        return buffer

    feed_received = lax.ppermute(feed(None), "tower", SWAP)
    feed_total = lax.all_to_all(feed(feed_received), "dp", 0, 0, tiled=True)

    backs = []
    for (t, name, ends, tokens, w, _), f, m, h in zip(towers, fronts, middles, heads):
        backs.append(back(t, name, ends, m[3], h[8], f[1], f[2], tokens, w[0], w[3], w[2]))

    vectors = []
    for m, h, k in zip(middles, heads, backs):
        vectors += [k[2], k[3], m[5], h[2], m[6], h[3], h[0], h[1]]

    def rest(received):
        buffer = None
        for (t, name, ends, _, _, _), f, k in zip(towers, fronts, backs):
            buffer = wide_weights(
                t, name + "_joint", place, ends, (f[0], f[3]), k[0], None, REST_UNITS, REST_AT[name], received, buffer
            )
        return misc(place, heads, vectors, received, buffer)

    rest_received = lax.ppermute(rest(None), "tower", SWAP)
    rest_total = lax.all_to_all(rest(rest_received), "dp", 0, 0, tiled=True)
    mine = [
        sum_blocks(feed_total, 9).reshape(-1, 128),
        sum_blocks(rest_total, 9).reshape(-1, 128),
    ]
    theirs = [lax.ppermute(m, "tower", SWAP) for m in mine]
    weight_outs = (
        ((12, 2304), F32),
        ((12, 768), F32),
        ((12, 3072), F32),
        ((48, 768), F32),
        ((12, 512), F32),
        ((8, 1536), F32),
        ((8, 512), F32),
        ((8, 2048), F32),
        ((32, 512), F32),
        ((8, 512), F32),
    )
    vector_outs = (((1, 12), F32),) * 6 + (((1, 8), F32),) * 6
    grads = call(unpack_kernel, "unpack", (place,), (*mine, *theirs), weight_outs + vector_outs)

    def ordered(vectors, weights):
        joint, output, widen, narrow, projection = weights
        v = [x.reshape(-1) for x in vectors]
        return [v[0], v[1], joint, output, v[2], v[3], widen, narrow, v[4], v[5], projection]

    def by_sequence(t, grad):
        return grad.reshape(t.length, BATCH, t.width).transpose(1, 0, 2)

    return (
        loss,
        units[0],
        units[1],
        by_sequence(IMAGE, backs[0][1]),
        *ordered(grads[10:16], grads[:5]),
        by_sequence(TEXT, backs[1][1]),
        *ordered(grads[16:22], grads[5:10]),
        scale_grad,
    )


def solution(mesh):
    spread = P(("tower", "dp"), None, None)
    weights = [P()] * 11
    placed = (spread, *weights, spread, spread, P(("tower", "dp")), *weights, spread, P())
    vector, matrix = P("dp"), P("dp", None)
    grads = [vector, vector, matrix, matrix, vector, vector, matrix, matrix, vector, vector, matrix]
    units = P(("tower", "dp"), None)
    return jax.shard_map(
        shards,
        mesh=mesh,
        in_specs=placed,
        out_specs=(P(), units, units, spread, *grads, spread, *grads, P()),
        check_vma=False,
    )
```

time: 2300 us -> 382 us (0.17)
  waiting for transfers between devices: 819 us -> 110 us
  blocking collectives: 726 us -> 28.9 us
  local copies, waits for them, and re-layouts: 288 us -> 5.04 us
  Pallas kernels: 0 us -> 205 us
  starting transfers between devices: 168 us -> 21.3 us
  matrix products: 146 us -> 0 us
  other arithmetic: 115 us -> 2.49 us
    reduce_scatter x6 -> x0, waiting for transfers between devices: 738 us -> none  [the longest x1 354 us: shards(): lax.psum_scatter(local[18], 'dp', scatter_dimension=0, tiled=True)]
    unnamed x4 -> x0, blocking collectives: 726 us -> none
    pallas_call x0 -> x24, Pallas kernels: none -> 205 us  [the longest x14 90.8 us: buffer_call(): pl.pallas_call(kernel, name=name, out_shape=jax.ShapeDtypeStruct((DEVS, u...]
    unnamed x64 -> x0, starting transfers between devices: 167 us -> none
    unnamed x282 -> x12, local copies, waits for them, and re-layouts: 161 us -> 4.41 us
    dot_general x45 -> x0, matrix products: 141 us -> none  [the longest x10 43.6 us: contract_rows(): lax.dot_general(left, right, (((0,), (0,)), ((), ())), preferred_element_...]
    all_to_all x0 -> x2, waiting for transfers between devices: none -> 89.3 us  [the longest x1 53.4 us: shards(): rest_total = lax.all_to_all(rest(rest_received), 'dp', 0, 0, tiled=True)]
    reshape x21 -> x0, local copies, waits for them, and re-layouts: 61.6 us -> none  [the longest x2 12.7 us: block_forward(): joint = joint.reshape(batch, length, 3, heads, head_size)]
  transfers between devices with their start and end apart: 74 -> 7, of which waited for: 7 -> 5; matrix products, arithmetic and copies ran while one was open for 31% -> 0% of each run, Pallas kernels for 0% -> 27%
where the time goes in v1:
time: 382 us; the launch traced here: 375 us
  Pallas kernels  205 us (54%)
  waiting for transfers between devices  110 us (29%)
  blocking collectives  28.9 us (8%)
  starting transfers between devices  21.3 us (6%)
  local copies, waits for them, and re-layouts  5.04 us (1%)
    pallas_call x14, Pallas kernels, buffer_call(): pl.pallas_call(kernel, name=name, out_shape=jax.ShapeDtypeStruct((DEVS, u...  90.8 us
    pallas_call x6, Pallas kernels, call(): pl.pallas_call(body, name=name, out_shape=tuple((jax.ShapeDtypeStruct(sha...  74.5 us
    all_to_all x1, waiting for transfers between devices, shards(): rest_total = lax.all_to_all(rest(rest_received), 'dp', 0, 0, tiled=True)  53.4 us
    all_to_all x1, waiting for transfers between devices, shards(): feed_total = lax.all_to_all(feed(feed_received), 'dp', 0, 0, tiled=True)  35.8 us
    pallas_call x2, Pallas kernels, middle(): pl.pallas_call(functools.partial(middle_kernel, t), name=name + '_middle'...  31.6 us
    all_to_all x1, blocking collectives, shards(): lax.all_to_all(jnp.broadcast_to(both[None], (DEVS, *both.shape)), 'dp', 0...  28.9 us
    ppermute x1, waiting for transfers between devices, shards(): feed_received = lax.ppermute(feed(None), 'tower', SWAP)  11.6 us
    all_to_all x1, starting transfers between devices, shards(): rest_total = lax.all_to_all(rest(rest_received), 'dp', 0, 0, tiled=True)  9.23 us
  transfers between devices with their start and end apart: 7, of which 5 were waited for; matrix products, arithmetic and copies ran while one was open for 0% of the time, Pallas kernels for 27%

profile of v1, /device:TPU:1, one launch (start us, length us, event | category | flops | bytes accessed | tf_op | source)
XLA Modules:
  0.0 374.8 jit_solution(4050117749793761484)
XLA Ops:
  0.7 1.2 broadcast_add_fusion.ends
  1.8 0.5 broadcast_3_ends.2.ends
  2.3 17.0 %image_front.1 = (bf16[400,768]{1,0:T(8,128)(2,1)}, bf16[8,64,2304]{2,1,0:T(8,128)(2,1)}, bf16[8,6,64,128]{3,2,1,0:T(8,128)(2,1)}, bf16[400,768]{1,0:T(8,128)(2,...) custom-call(s32[8]{0:T(128)} %broadcast_3_ends.2.ends, ...), custom_call_target="tpu_custom_call" | custom-call | flops 4294967296 | bytes 20971520 | tf_op jit(solution)/shard_map/image_front/pallas_call | solution.py:907
  19.4 0.0 copy-start.3
  19.4 13.6 %text_front.1 = (bf16[640,512]{1,0:T(8,128)(2,1)}, bf16[8,80,1536]{2,1,0:T(8,128)(2,1)}, bf16[8,4,80,160]{3,2,1,0:T(8,128)(2,1)}, bf16[640,512]{1,0:T(8,128)(2,1...) custom-call(s32[8]{0:T(128)} %broadcast_add_fusion.ends, ...), custom_call_target="tpu_custom_call" | custom-call | flops 4294967296 | bytes 20971520 | tf_op jit(solution)/shard_map/text_front/pallas_call | solution.py:907
  33.0 0.7 pad_maximum_fusion
  33.7 0.1 broadcast_in_dim.2
  33.8 28.9 %all_to_all.15 = bf16[64,8,1024]{2,1,0:T(8,128)(2,1)S(1)} all-to-all(bf16[64,8,1024]{2,1,0:T(8,128)(2,1)S(1)} %broadcast_in_dim.2), channel_id=1, replica_groups=mesh['tower'=2,'dp'=64] {'dp'}, dimensions={0} | all-to-all | bytes 2097152 | tf_op jit(solution)/shard_map/all_to_all | solution.py:1025
  62.8 2.7 collective-permute-start
  65.4 17.8 %image_middle.1 = (bf16[400,768]{1,0:T(8,128)(2,1)}, bf16[400,3072]{1,0:T(8,128)(2,1)}, bf16[400,3072]{1,0:T(8,128)(2,1)}, f32[400,768]{1,0:T(8,128)}, f32[8,768...) custom-call(s32[8]{0:T(128)} %broadcast_3_ends.2.ends, f32[400,768]{1,0:T(8,128)} %get-tuple-element.118.mixed, ...), custom_call_target="tpu_custom_call" | custom-call | flops 8589934592 | bytes 20971520 | tf_op jit(solution)/shard_map/image_middle/pallas_call | solution.py:963
  83.8 0.6 pad_add_fusion.place
  84.5 13.8 %text_middle.1 = (bf16[640,512]{1,0:T(8,128)(2,1)}, bf16[640,2048]{1,0:T(8,128)(2,1)}, bf16[640,2048]{1,0:T(8,128)(2,1)}, f32[640,512]{1,0:T(8,128)}, f32[8,512]...) custom-call(s32[8]{0:T(128)} %broadcast_add_fusion.ends, f32[640,512]{1,0:T(8,128)} %get-tuple-element.124.mixed, ...), custom_call_target="tpu_custom_call" | custom-call | flops 8589934592 | bytes 20971520 | tf_op jit(solution)/shard_map/text_middle/pallas_call | solution.py:963
  98.3 0.0 copy-start.2
  98.3 1.0 copy-done.2
  99.2 15.3 %pairs.1 = (f32[1,128]{1,0:T(1,128)}, f32[1,128]{1,0:T(1,128)}, f32[1,768]{1,0:T(1,128)}, f32[1,768]{1,0:T(1,128)}, f32[1,768]{1,0:T(1,128)}, /*index=5*/f32[1,7...) custom-call(s32[2]{0:T(128)} %pad_add_fusion.place, ...), custom_call_target="tpu_custom_call" | custom-call | flops 4294967296 | bytes 20971520 | tf_op jit(solution)/shard_map/pairs/pallas_call | solution.py:907
  114.5 8.2 %image_widen.2.refs_0_ = bf16[64,27,16,128]{3,2,1,0:T(8,128)(2,1)} custom-call(s32[2]{0:T(128)} %pad_add_fusion.place, s32[8]{0:T(128)} %broadcast_3_ends.2.ends, bf16[400,768]{1,0:T(8,128)(2,1)} %get-tuple-element.139.refs_0_, bf16[400,3072]{1,0:T(8,128)(2,1)} %get-tuple-element.140.refs_1_.refs_2_, bf16[400,3072]{1,0:T(8,128)(2,1)} %get-tuple-element.140.refs_1_.refs_2_, ...), custom_call_target="tpu_custom_call" | custom-call | flops 1887436800 | bytes 8388608 | tf_op jit(solution)/shard_map/image_widen/pallas_call | solution.py:651
  122.7 7.6 %image_narrow.2.refs_3_ = bf16[64,27,16,128]{3,2,1,0:T(8,128)(2,1)} custom-call(s32[2]{0:T(128)} %pad_add_fusion.place, s32[8]{0:T(128)} %broadcast_3_ends.2.ends, bf16[400,3072]{1,0:T(8,128)(2,1)} %get-tuple-element.137.active, bf16[400,768]{1,0:T(8,128)(2,1)} %bitcast.45, f32[8,768]{1,0:T(8,128)} %get-tuple-element.138.new, ...), custom_call_target="tpu_custom_call", output_to_operand_aliasing={{}: (5, {})} | custom-call | flops 1887436800 | bytes 8388608 | tf_op jit(solution)/shard_map/image_narrow/pallas_call | solution.py:651
  130.4 5.2 %text_widen.2.refs_0_ = bf16[64,27,16,128]{3,2,1,0:T(8,128)(2,1)} custom-call(s32[2]{0:T(128)} %pad_add_fusion.place, s32[8]{0:T(128)} %broadcast_add_fusion.ends, bf16[640,512]{1,0:T(8,128)(2,1)} %get-tuple-element.134.refs_0_, bf16[640,2048]{1,0:T(8,128)(2,1)} %get-tuple-element.135.refs_1_, ...), custom_call_target="tpu_custom_call", output_to_operand_aliasing={{}: (5, {})} | custom-call | flops 1342177280 | bytes 8388608 | tf_op jit(solution)/shard_map/text_widen/pallas_call | solution.py:651
  135.6 6.4 %text_narrow.2 = bf16[64,27,16,128]{3,2,1,0:T(8,128)(2,1)} custom-call(s32[2]{0:T(128)} %pad_add_fusion.place, s32[8]{0:T(128)} %broadcast_add_fusion.ends, bf16[640,2048]{1,0:T(8,128)(2,1)} %get-tuple-element.132.active, bf16[616,512]{1,0:T(8,128)(2,1)} %bitcast.42, f32[8,512]{1,0:T(8,128)} %get-tuple-element.133.new, ...), custom_call_target="tpu_custom_call", output_to_operand_aliasing={{}: (5, {})} | custom-call | flops 1342177280 | bytes 8388608 | tf_op jit(solution)/shard_map/text_narrow/pallas_call | solution.py:651
  142.0 0.0 collective-permute-start.1
  142.0 11.6 %collective-permute-done.1.refs_5_.refs_0_.refs_3_ = bf16[64,27,16,128]{3,2,1,0:T(8,128)(2,1)} collective-permute-done((bf16[64,27,16,128]{3,2,1,0:T(8,128)(2,1)}, bf16[64,27,16,128]{3,2,1,0:T(8,128)(2,1)}, u32[]{:S(2)}, u32[]{:S(2)}) %collective-permute-start.1) | collective-permute-done | bytes 7077920 | tf_op jit(solution)/shard_map/ppermute | solution.py:1063
  153.6 8.7 %image_widen.3.refs_1_ = bf16[64,27,16,128]{3,2,1,0:T(8,128)(2,1)} custom-call(s32[2]{0:T(128)} %pad_add_fusion.place, s32[8]{0:T(128)} %broadcast_3_ends.2.ends, bf16[400,768]{1,0:T(8,128)(2,1)} %get-tuple-element.139.refs_0_, bf16[400,3072]{1,0:T(8,128)(2,1)} %get-tuple-element.140.refs_1_.refs_2_, bf16[400,3072]{1,0:T(8,128)(2,1)} %get-tuple-element.140.refs_1_.refs_2_, ...), custom_call_target="tpu_custom_call" | custom-call | flops 1887436800 | bytes 8388608 | tf_op jit(solution)/shard_map/image_widen/pallas_call | solution.py:651
  162.4 8.2 %image_narrow.3.refs_4_ = bf16[64,27,16,128]{3,2,1,0:T(8,128)(2,1)} custom-call(s32[2]{0:T(128)} %pad_add_fusion.place, s32[8]{0:T(128)} %broadcast_3_ends.2.ends, bf16[400,3072]{1,0:T(8,128)(2,1)} %get-tuple-element.137.active, bf16[400,768]{1,0:T(8,128)(2,1)} %bitcast.46, f32[8,768]{1,0:T(8,128)} %get-tuple-element.138.new, ...), custom_call_target="tpu_custom_call", output_to_operand_aliasing={{}: (6, {})} | custom-call | flops 1887436800 | bytes 8388608 | tf_op jit(solution)/shard_map/image_narrow/pallas_call | solution.py:651
  170.6 5.3 %text_widen.3.refs_1_ = bf16[64,27,16,128]{3,2,1,0:T(8,128)(2,1)} custom-call(s32[2]{0:T(128)} %pad_add_fusion.place, s32[8]{0:T(128)} %broadcast_add_fusion.ends, bf16[640,512]{1,0:T(8,128)(2,1)} %get-tuple-element.134.refs_0_, bf16[640,2048]{1,0:T(8,128)(2,1)} %get-tuple-element.135.refs_1_, ...), custom_call_target="tpu_custom_call", output_to_operand_aliasing={{}: (6, {})} | custom-call | flops 1342177280 | bytes 8388608 | tf_op jit(solution)/shard_map/text_widen/pallas_call | solution.py:651
  175.8 6.7 %text_narrow.3 = bf16[64,27,16,128]{3,2,1,0:T(8,128)(2,1)} custom-call(s32[2]{0:T(128)} %pad_add_fusion.place, s32[8]{0:T(128)} %broadcast_add_fusion.ends, bf16[640,2048]{1,0:T(8,128)(2,1)} %get-tuple-element.132.active, bf16[616,512]{1,0:T(8,128)(2,1)} %bitcast.43, f32[8,512]{1,0:T(8,128)} %get-tuple-element.133.new, ...), custom_call_target="tpu_custom_call", output_to_operand_aliasing={{}: (6, {})} | custom-call | flops 1342177280 | bytes 8388608 | tf_op jit(solution)/shard_map/text_narrow/pallas_call | solution.py:651
  182.5 5.7 %all-to-all-start.1 = ((bf16[64,27,16,128]{3,2,1,0:T(8,128)(2,1)}), bf16[64,27,16,128]{3,2,1,0:T(8,128)(2,1)}, u32[]{:S(2)}, u32[]{:S(2)}) async-start(bf16[64,27,16,128]{3,2,1,0:T(8,128)(2,1)} %text_narrow.3), calls=%async_computation.1 | async-start | bytes 14155776 | tf_op jit(solution)/shard_map/all_to_all | solution.py:1064
  188.2 14.1 %image_back.1 = (bf16[400,3072]{1,0:T(8,128)(2,1)}, f32[400,768]{1,0:T(8,128)}, f32[1,768]{1,0:T(1,128)}, f32[1,768]{1,0:T(1,128)}) custom-call(s32[8]{0:T(128)} %broadcast_3_ends.2.ends, f32[400,768]{1,0:T(8,128)} %get-tuple-element.127.mixed_grad, f32[8,768]{1,0:T(8,128)} %get-tuple-element.128.mixed_grad_row, ...), custom_call_target="tpu_custom_call" | custom-call | flops 8589934592 | bytes 20971520 | tf_op jit(solution)/shard_map/image_back/pallas_call | solution.py:907
  202.3 7.3 %image_joint.2.refs_3_ = bf16[64,18,16,128]{3,2,1,0:T(8,128)(2,1)} custom-call(s32[2]{0:T(128)} %pad_add_fusion.place, s32[8]{0:T(128)} %broadcast_3_ends.2.ends, bf16[400,768]{1,0:T(8,128)(2,1)} %get-tuple-element.169.refs_0_, bf16[400,768]{1,0:T(8,128)(2,1)} %get-tuple-element.170.refs_1_, bf16[400,3072]{1,0:T(8,128)(2,1)} %get-tuple-element.171.refs_2_.refs_3_, ...), custom_call_target="tpu_custom_call" | custom-call | flops 1887436800 | bytes 8388608 | tf_op jit(solution)/shard_map/image_joint/pallas_call | solution.py:651
  209.5 12.2 %text_back.1 = (bf16[640,2048]{1,0:T(8,128)(2,1)}, f32[616,512]{1,0:T(8,128)}, f32[1,512]{1,0:T(1,128)}, f32[1,512]{1,0:T(1,128)}) custom-call(s32[8]{0:T(128)} %broadcast_add_fusion.ends, f32[640,512]{1,0:T(8,128)} %get-tuple-element.154.mixed_grad, f32[8,512]{1,0:T(8,128)} %get-tuple-element.155.mixed_grad_row, ...), custom_call_target="tpu_custom_call" | custom-call | flops 8589934592 | bytes 20971520 | tf_op jit(solution)/shard_map/text_back/pallas_call | solution.py:907
  221.7 5.3 %text_joint.2.refs_4_ = bf16[64,18,16,128]{3,2,1,0:T(8,128)(2,1)} custom-call(s32[2]{0:T(128)} %pad_add_fusion.place, s32[8]{0:T(128)} %broadcast_add_fusion.ends, bf16[640,512]{1,0:T(8,128)(2,1)} %get-tuple-element.166.refs_0_, bf16[640,512]{1,0:T(8,128)(2,1)} %get-tuple-element.167.refs_1_, ...), custom_call_target="tpu_custom_call", output_to_operand_aliasing={{}: (5, {})} | custom-call | flops 1342177280 | bytes 8388608 | tf_op jit(solution)/shard_map/text_joint/pallas_call | solution.py:651
  227.0 3.3 misc.2
  230.3 0.4 collective-permute-start.2
  230.7 8.0 %collective-permute-done.2.refs_4_.refs_3_.refs_20_ = bf16[64,18,16,128]{3,2,1,0:T(8,128)(2,1)S(1)} collective-permute-done((bf16[64,18,16,128]{3,2,1,0:T(8,128)(2,1)}, bf16[64,18,16,128]{3,2,1,0:T(8,128)(2,1)S(1)}, u32[]{:S(2)}, u32[]{:S(2)}) %collective-permute-start.2) | collective-permute-done | bytes 4718624 | tf_op jit(solution)/shard_map/ppermute | solution.py:1082
  238.6 2.1 copy-done
  240.7 8.0 %image_joint.3.refs_4_ = bf16[64,18,16,128]{3,2,1,0:T(8,128)(2,1)} custom-call(s32[2]{0:T(128)} %pad_add_fusion.place, s32[8]{0:T(128)} %broadcast_3_ends.2.ends, bf16[400,768]{1,0:T(8,128)(2,1)} %get-tuple-element.169.refs_0_, bf16[400,768]{1,0:T(8,128)(2,1)} %get-tuple-element.170.refs_1_, bf16[400,3072]{1,0:T(8,128)(2,1)} %get-tuple-element.171.refs_2_.refs_3_, ...), custom_call_target="tpu_custom_call" | custom-call | flops 1887436800 | bytes 8388608 | tf_op jit(solution)/shard_map/image_joint/pallas_call | solution.py:651
  248.7 5.5 %text_joint.3.refs_21_ = bf16[64,18,16,128]{3,2,1,0:T(8,128)(2,1)} custom-call(s32[2]{0:T(128)} %pad_add_fusion.place, s32[8]{0:T(128)} %broadcast_add_fusion.ends, bf16[640,512]{1,0:T(8,128)(2,1)} %get-tuple-element.166.refs_0_, bf16[640,512]{1,0:T(8,128)(2,1)} %get-tuple-element.167.refs_1_, ...), custom_call_target="tpu_custom_call", output_to_operand_aliasing={{}: (6, {})} | custom-call | flops 1342177280 | bytes 8388608 | tf_op jit(solution)/shard_map/text_joint/pallas_call | solution.py:651
  254.2 5.1 %misc.3 = bf16[64,18,16,128]{3,2,1,0:T(8,128)(2,1)} custom-call(s32[2]{0:T(128)} %pad_add_fusion.place, f32[8,768]{1,0:T(8,128)} %get-tuple-element.142.refs_0_, f32[8,512]{1,0:T(8,128)} %get-tuple-element.143.refs_1_, f32[8,512]{1,0:T(8,128)} %get-tuple-element.144.refs_2_, f32[8,512]{1,0:T(8,128)} %get-tuple-element.145.refs_3_, ...), custom_call_target="tpu_custom_call", output_to_operand_aliasing={{}: (22, {})} | custom-call | flops 268435456 | bytes 8388608 | tf_op jit(solution)/shard_map/misc/pallas_call | solution.py:651
  259.3 35.8 %all-to-all-done.1.received = bf16[64,27,16,128]{3,2,1,0:T(8,128)(2,1)} async-done(((bf16[64,27,16,128]{3,2,1,0:T(8,128)(2,1)}), bf16[64,27,16,128]{3,2,1,0:T(8,128)(2,1)}, u32[]{:S(2)}, u32[]{:S(2)}) %all-to-all-start.1) | async-done | bytes 7077920 | tf_op jit(solution)/shard_map/all_to_all | solution.py:1064
  295.1 9.2 %all-to-all-start.2 = ((bf16[64,18,16,128]{3,2,1,0:T(8,128)(2,1)}), bf16[64,18,16,128]{3,2,1,0:T(8,128)(2,1)}, u32[]{:S(2)}, u32[]{:S(2)}) async-start(bf16[64,18,16,128]{3,2,1,0:T(8,128)(2,1)} %misc.3), calls=%async_computation.2 | async-start | bytes 9437184 | tf_op jit(solution)/shard_map/all_to_all | solution.py:1083
  304.4 4.9 %sum_blocks.2 = f32[27,16,128]{2,1,0:T(8,128)} custom-call(bf16[64,27,16,128]{3,2,1,0:T(8,128)(2,1)} %all-to-all-done.1.received), custom_call_target="tpu_custom_call" | custom-call | tf_op jit(solution)/shard_map/sum_blocks/pallas_call | solution.py:810
  309.2 1.2 collective-permute-start.3
  310.4 53.4 %all-to-all-done.2.received = bf16[64,18,16,128]{3,2,1,0:T(8,128)(2,1)} async-done(((bf16[64,18,16,128]{3,2,1,0:T(8,128)(2,1)}), bf16[64,18,16,128]{3,2,1,0:T(8,128)(2,1)}, u32[]{:S(2)}, u32[]{:S(2)}) %all-to-all-start.2) | async-done | bytes 4718624 | tf_op jit(solution)/shard_map/all_to_all | solution.py:1083
  363.9 3.4 sum_blocks.3
  367.2 2.1 collective-permute-start.4
  369.3 1.2 collective-permute-done.4.rest_other
  370.6 0.7 copy-done.5
  371.2 0.7 copy-done.4
  371.9 2.4 unpack.1
  (8 shorter events, 0.0 us)
Async XLA Ops:
  19.4 13.6 %copy-start.3 = (bf16[8,512]{1,0:T(8,128)(2,1)S(1)}, bf16[8,512]{1,0:T(8,128)(2,1)}, u32[]{:S(2)}) copy-start(bf16[8,512]{1,0:T(8,128)(2,1)} %get-tuple-element.85.image_unit) | copy-start | bytes 24580
  62.8 20.4 %copy-start.1 = (bf16[64,8,1024]{2,1,0:T(8,128)(2,1)}, bf16[64,8,1024]{2,1,0:T(8,128)(2,1)S(1)}, u32[]{:S(2)}) copy-start(bf16[64,8,1024]{2,1,0:T(8,128)(2,1)S(1)} %all_to_all.15) | copy-start | bytes 3145732
  62.8 35.5 %collective-permute-start = (bf16[512,1024]{1,0:T(8,128)(2,1)S(1)}, bf16[512,1024]{1,0:T(8,128)(2,1)S(1)}, u32[]{:S(2)}, u32[]{:S(2)}) collective-permute-start(bf16[512,1024]{1,0:T(8,128)(2,1)S(1)} %bitcast.39), channel_id=1, source_target_pairs={{0,64},{64,0},{1,65},{65,1},{2,66},{66,2},{3,67},{67,3},{4,68},{68... | collective-permute-start | bytes 3145736 | tf_op jit(solution)/shard_map/ppermute | solution.py:1028
  98.3 1.0 copy-start.2
  142.0 11.6 %collective-permute-start.1 = (bf16[64,27,16,128]{3,2,1,0:T(8,128)(2,1)}, bf16[64,27,16,128]{3,2,1,0:T(8,128)(2,1)}, u32[]{:S(2)}, u32[]{:S(2)}) collective-permute-start(bf16[64,27,16,128]{3,2,1,0:T(8,128)(2,1)} %text_narrow.2), channel_id=1, source_target_pairs={{0,64},{64,0},{1,65},{65,1},{2,66},{66,2},{3,67},{67,3},{4,68},{68... | collective-permute-start | bytes 21233672 | tf_op jit(solution)/shard_map/ppermute | solution.py:1063
  182.5 112.7 %all-to-all-start.1 = ((bf16[64,27,16,128]{3,2,1,0:T(8,128)(2,1)}), bf16[64,27,16,128]{3,2,1,0:T(8,128)(2,1)}, u32[]{:S(2)}, u32[]{:S(2)}) async-start(bf16[64,27,16,128]{3,2,1,0:T(8,128)(2,1)} %text_narrow.3), calls=%async_computation.1 | async-start | bytes 14155776 | tf_op jit(solution)/shard_map/all_to_all | solution.py:1064
  230.3 8.4 %collective-permute-start.2 = (bf16[64,18,16,128]{3,2,1,0:T(8,128)(2,1)}, bf16[64,18,16,128]{3,2,1,0:T(8,128)(2,1)S(1)}, u32[]{:S(2)}, u32[]{:S(2)}) collective-permute-start(bf16[64,18,16,128]{3,2,1,0:T(8,128)(2,1)} %misc.2), channel_id=1, source_target_pairs={{0,64},{64,0},{1,65},{65,1},{2,66},{66,2},{3,67},{67,3},{4,68},{68... | collective-permute-start | bytes 14155784 | tf_op jit(solution)/shard_map/ppermute | solution.py:1082
  238.6 2.1 copy-start
  295.1 68.7 %all-to-all-start.2 = ((bf16[64,18,16,128]{3,2,1,0:T(8,128)(2,1)}), bf16[64,18,16,128]{3,2,1,0:T(8,128)(2,1)}, u32[]{:S(2)}, u32[]{:S(2)}) async-start(bf16[64,18,16,128]{3,2,1,0:T(8,128)(2,1)} %misc.3), calls=%async_computation.2 | async-start | bytes 9437184 | tf_op jit(solution)/shard_map/all_to_all | solution.py:1083
  309.2 61.3 %collective-permute-start.3 = (f32[432,128]{1,0:T(8,128)}, f32[432,128]{1,0:T(8,128)S(1)}, u32[]{:S(2)}, u32[]{:S(2)}) collective-permute-start(f32[432,128]{1,0:T(8,128)} %bitcast.47), channel_id=1, source_target_pairs={{0,64},{64,0},{1,65},{65,1},{2,66},{66,2},{3,67},{67,3},{4,68},{68... | collective-permute-start | bytes 663560 | tf_op jit(solution)/shard_map/ppermute | solution.py:1088
  367.2 3.3 collective-permute-start.4
  370.6 0.7 copy-start.5
  371.2 0.7 copy-start.4
